TPU v7x, 32 devices: a whole 2x2x4 slice. The times are simulated.
32 devices in a mesh: dp: 8 (over y, x, core), mp: 4 (over z).
Axes of the slice: x: 2, y: 2, z: 4, core: 2. Of those that a mesh axis runs over, the one named last changes fastest.
Arguments:
- inputs: float32 [8192, 1024], P(('dp', 'mp')), may hold values from -6 to 6
- doc_ids: int32 [8, 1024], P('dp'), may hold values from 0 to 7, never falling along the last dimension, each value on 1 to 768 neighbouring positions
- cotangent: float32 [8192, 1024], P(('dp', 'mp')), may hold values from -6 to 6
- norm1_gain: float32 [1024], replicated, may hold values from 0.25 to 1.75
- norm2_gain: float32 [1024], replicated, may hold values from 0.25 to 1.75
- qnorm_gain: float32 [64], replicated, may hold values from 0.25 to 1.75
- knorm_gain: float32 [64], replicated, may hold values from 0.25 to 1.75
- q_weight: bfloat16 [1024, 1024], P(None, 'mp'), may hold values from -0.1875 to 0.1875
- k_weight: bfloat16 [1024, 512], P(None, 'mp'), may hold values from -0.1875 to 0.1875
- v_weight: bfloat16 [1024, 512], P(None, 'mp'), may hold values from -0.1875 to 0.1875
- o_weight: bfloat16 [1024, 1024], P('mp'), may hold values from -0.75 to 0.75
- gate_weight: bfloat16 [1024, 4608], P(None, 'mp'), may hold values from -0.1875 to 0.1875
- up_weight: bfloat16 [1024, 4608], P(None, 'mp'), may hold values from -0.1875 to 0.1875
- down_weight: bfloat16 [4608, 1024], P('mp'), may hold values from -0.09375 to 0.09375
Outputs:
- result: float32 [8192, 1024], P(('dp', 'mp'))
- inputs_grad: float32 [8192, 1024], P(('dp', 'mp'))
- norm1_grad: float32 [1024], replicated
- norm2_grad: float32 [1024], replicated
- qnorm_grad: float32 [64], replicated
- knorm_grad: float32 [64], replicated
- q_grad: float32 [1024, 1024], P(None, 'mp')
- k_grad: float32 [1024, 512], P(None, 'mp')
- v_grad: float32 [1024, 512], P(None, 'mp')
- o_grad: float32 [1024, 1024], P('mp')
- gate_grad: float32 [1024, 4608], P(None, 'mp')
- up_grad: float32 [1024, 4608], P(None, 'mp')
- down_grad: float32 [4608, 1024], P('mp')
Inputs may be any that keep to these rules, and one draw needn't show every extreme that they name: `doc_ids`: numbers start at 0 in each sequence and never fall along it; each document has 1 to 768 tokens, some exactly 768.
All inputs are finite; a program needn't handle non-finite values.
Results may differ from a plain program's by a relative error of at most 0.018.
Values may be sent and summed in bfloat16 or wider, within the bound.
A program may use at most 128 MiB of HBM per device.

v0:
```python
import jax
import jax.numpy as jnp
from jax import lax
from jax.sharding import PartitionSpec as P

HEAD = 64


EPS = 1e-05
THETA = 1000000.0


def normed(field, weights):
    return field * lax.rsqrt(jnp.mean(field * field, -1, keepdims=True) + EPS) * weights


def positions(doc_row):
    length_all = doc_row.shape[0]
    positions_all = jnp.arange(length_all, dtype=jnp.int32)
    previous = jnp.concatenate([doc_row[:1] - 1, doc_row[:-1]])
    doc_starts = jnp.where(doc_row != previous, positions_all, 0)
    return positions_all - lax.cummax(doc_starts)


def rotate(field, where_at):
    half_dim = HEAD // 2
    frequency = THETA ** (-jnp.arange(half_dim, dtype=jnp.float32) * 2.0 / HEAD)
    angles = where_at.astype(jnp.float32)[:, None] * frequency[None, :]
    cosine = jnp.cos(angles)[:, None, :]
    sine_val = jnp.sin(angles)[:, None, :]
    first_half = field[..., :half_dim]
    second_half = field[..., half_dim:]
    return jnp.concatenate(
        [
            first_half * cosine - second_half * sine_val,
            second_half * cosine + first_half * sine_val,
        ],
        -1,
    )


def gated(gate_pre, up_pre):
    return jax.nn.silu(gate_pre) * up_pre


def dot_plain(left, right):
    return jnp.dot(left, right, preferred_element_type=jnp.float32)


def dot_left_t(left, right):
    return lax.dot_general(
        left, right, (((0,), (0,)), ((), ())), preferred_element_type=jnp.float32
    )


def dot_right_t(left, right):
    return lax.dot_general(
        left, right, (((1,), (1,)), ((), ())), preferred_element_type=jnp.float32
    )


def body(
    inputs,
    doc_ids,
    cotangent,
    norm1_gain,
    norm2_gain,
    qnorm_gain,
    knorm_gain,
    q_weight,
    k_weight,
    v_weight,
    o_weight,
    gate_weight,
    up_weight,
    down_weight,
):
    doc_full = doc_ids[0]
    full_len = doc_full.shape[0]
    where_full = positions(doc_full)
    key_ids = jnp.arange(full_len, dtype=jnp.int32)
    query_cols = q_weight.shape[1]
    key_cols = k_weight.shape[1]
    query_heads = query_cols // HEAD
    kv_heads = key_cols // HEAD
    group_size = query_heads // kv_heads
    score_scale = HEAD ** (-0.5)
    block_rows = min(512, full_len)
    block_count = full_len // block_rows
    block_starts = jnp.arange(block_count, dtype=jnp.int32) * block_rows
    normed_one, norm1_back = jax.vjp(normed, inputs, norm1_gain)
    hidden = lax.all_gather(normed_one.astype(jnp.bfloat16), "mp", axis=0, tiled=True)
    joined = jnp.concatenate([q_weight, k_weight, v_weight], 1)
    projected = dot_plain(hidden, joined)
    query_raw = projected[:, :query_cols].reshape(full_len, query_heads, HEAD)
    key_raw = projected[:, query_cols : query_cols + key_cols].reshape(full_len, kv_heads, HEAD)
    values_all = (
        projected[:, query_cols + key_cols :].astype(jnp.bfloat16).reshape(full_len, kv_heads, HEAD)
    )
    query_rot, query_back = jax.vjp(
        lambda raw_in, weights: rotate(normed(raw_in, weights), where_full), query_raw, qnorm_gain
    )
    key_rot, key_back = jax.vjp(
        lambda raw_in, weights: rotate(normed(raw_in, weights), where_full), key_raw, knorm_gain
    )
    queries = query_rot.astype(jnp.bfloat16).reshape(full_len, kv_heads, group_size, HEAD)
    keys_all = key_rot.astype(jnp.bfloat16)

    def scores_of(begin_row):
        query_block = lax.dynamic_slice_in_dim(queries, begin_row, block_rows, 0)
        raw_scores = (
            jnp.einsum("qkgd,skd->kgqs", query_block, keys_all, preferred_element_type=jnp.float32)
            * score_scale
        )
        row_ids = begin_row + jnp.arange(block_rows, dtype=jnp.int32)
        doc_block = lax.dynamic_slice_in_dim(doc_full, begin_row, block_rows, 0)
        allowed = (doc_block[:, None] == doc_full[None, :]) & (key_ids[None, :] <= row_ids[:, None])
        return (jnp.where(allowed, raw_scores, -1e30), query_block)

    def forward_block(begin_row):
        scores, query_block = scores_of(begin_row)
        row_max = jnp.max(scores, -1, keepdims=True)
        exponent = jnp.exp(scores - row_max)
        row_total = jnp.sum(exponent, -1, keepdims=True)
        probs = (exponent / row_total).astype(jnp.bfloat16)
        block_out = jnp.einsum(
            "kgqs,skd->qkgd", probs, values_all, preferred_element_type=jnp.float32
        )
        return (block_out, (row_max + jnp.log(row_total))[..., 0])

    block_out, log_totals = lax.map(forward_block, block_starts)
    attended = block_out.reshape(full_len, query_cols).astype(jnp.bfloat16)
    mid_rows = inputs + lax.psum_scatter(
        dot_plain(attended, o_weight), "mp", scatter_dimension=0, tiled=True
    )
    normed_two, norm2_back = jax.vjp(normed, mid_rows, norm2_gain)
    hidden_mid = lax.all_gather(normed_two.astype(jnp.bfloat16), "mp", axis=0, tiled=True)
    gate_pre = dot_plain(hidden_mid, gate_weight)
    up_pre = dot_plain(hidden_mid, up_weight)
    activated, gated_back = jax.vjp(gated, gate_pre, up_pre)
    act_low = activated.astype(jnp.bfloat16)
    result = mid_rows + lax.psum_scatter(
        dot_plain(act_low, down_weight).astype(jnp.bfloat16), "mp", scatter_dimension=0, tiled=True
    ).astype(jnp.float32)
    grad_full = lax.all_gather(cotangent.astype(jnp.bfloat16), "mp", axis=0, tiled=True)
    grad_act = dot_right_t(grad_full, down_weight)
    down_wgrad = dot_left_t(act_low, grad_full)
    grad_gate, grad_up = gated_back(grad_act)
    grad_gate = grad_gate.astype(jnp.bfloat16)
    grad_up = grad_up.astype(jnp.bfloat16)
    gate_wgrad = dot_left_t(hidden_mid, grad_gate)
    up_wgrad = dot_left_t(hidden_mid, grad_up)
    grad_normed_mid = lax.psum_scatter(
        dot_right_t(grad_gate, gate_weight) + dot_right_t(grad_up, up_weight),
        "mp",
        scatter_dimension=0,
        tiled=True,
    )
    grad_mid_norm, gain2_grad = norm2_back(grad_normed_mid)
    grad_mid = cotangent + grad_mid_norm
    grad_mid_full = lax.all_gather(grad_mid.astype(jnp.bfloat16), "mp", axis=0, tiled=True)
    grad_att = (
        dot_right_t(grad_mid_full, o_weight)
        .astype(jnp.bfloat16)
        .reshape(full_len, kv_heads, group_size, HEAD)
    )
    out_wgrad = dot_left_t(attended, grad_mid_full)

    def backward_block(carried, block_in):
        grad_keys, grad_values = carried
        begin_row, log_block = block_in
        scores, query_block = scores_of(begin_row)
        probs = jnp.exp(scores - log_block[..., None])
        grad_out = lax.dynamic_slice_in_dim(grad_att, begin_row, block_rows, 0)
        grad_probs = jnp.einsum(
            "qkgd,skd->kgqs", grad_out, values_all, preferred_element_type=jnp.float32
        )
        row_delta = jnp.sum(probs * grad_probs, -1, keepdims=True)
        grad_scores = (probs * (grad_probs - row_delta)).astype(jnp.bfloat16)
        grad_query = (
            jnp.einsum("kgqs,skd->qkgd", grad_scores, keys_all, preferred_element_type=jnp.float32)
            * score_scale
        )
        grad_keys = (
            grad_keys
            + jnp.einsum(
                "kgqs,qkgd->skd", grad_scores, query_block, preferred_element_type=jnp.float32
            )
            * score_scale
        )
        grad_values = grad_values + jnp.einsum(
            "kgqs,qkgd->skd",
            probs.astype(jnp.bfloat16),
            grad_out,
            preferred_element_type=jnp.float32,
        )
        return ((grad_keys, grad_values), grad_query)

    zero_kv = jnp.zeros((full_len, kv_heads, HEAD), jnp.float32)
    (grad_keys, grad_values), grad_queries = lax.scan(
        backward_block, (zero_kv, zero_kv), (block_starts, log_totals)
    )
    grad_qraw, qgain_grad = query_back(grad_queries.reshape(full_len, query_heads, HEAD))
    grad_kraw, kgain_grad = key_back(grad_keys)
    grad_joined = jnp.concatenate(
        [
            grad_qraw.reshape(full_len, query_cols),
            grad_kraw.reshape(full_len, key_cols),
            grad_values.reshape(full_len, key_cols),
        ],
        1,
    ).astype(jnp.bfloat16)
    joined_wgrad = dot_left_t(hidden, grad_joined)
    grad_normed_in = lax.psum_scatter(
        dot_right_t(grad_joined, joined).astype(jnp.bfloat16), "mp", scatter_dimension=0, tiled=True
    ).astype(jnp.float32)
    grad_in_norm, gain1_grad = norm1_back(grad_normed_in)
    inputs_grad = grad_mid + grad_in_norm
    gain_totals = lax.psum((gain1_grad, gain2_grad, qgain_grad, kgain_grad), ("dp", "mp"))
    joined_wgrad, out_wgrad, gate_wgrad, up_wgrad, down_wgrad = (
        lax.psum(joined_wgrad.astype(jnp.bfloat16), "dp").astype(jnp.float32),
        lax.psum(out_wgrad.astype(jnp.bfloat16), "dp").astype(jnp.float32),
        lax.psum(gate_wgrad.astype(jnp.bfloat16), "dp").astype(jnp.float32),
        lax.psum(up_wgrad.astype(jnp.bfloat16), "dp").astype(jnp.float32),
        lax.psum(down_wgrad.astype(jnp.bfloat16), "dp").astype(jnp.float32),
    )
    query_wgrad = joined_wgrad[:, :query_cols]
    key_wgrad = joined_wgrad[:, query_cols : query_cols + key_cols]
    value_wgrad = joined_wgrad[:, query_cols + key_cols :]
    return (
        result,
        inputs_grad,
        gain_totals[0],
        gain_totals[1],
        gain_totals[2],
        gain_totals[3],
        query_wgrad,
        key_wgrad,
        value_wgrad,
        out_wgrad,
        gate_wgrad,
        up_wgrad,
        down_wgrad,
    )


def solution(mesh):
    in_specs = (
        P(("dp", "mp"), None),
        P("dp", None),
        P(("dp", "mp"), None),
        P(),
        P(),
        P(),
        P(),
        P(None, "mp"),
        P(None, "mp"),
        P(None, "mp"),
        P("mp", None),
        P(None, "mp"),
        P(None, "mp"),
        P("mp", None),
    )
    out_specs = (
        P(("dp", "mp"), None),
        P(("dp", "mp"), None),
        P(),
        P(),
        P(),
        P(),
        P(None, "mp"),
        P(None, "mp"),
        P(None, "mp"),
        P("mp", None),
        P(None, "mp"),
        P(None, "mp"),
        P("mp", None),
    )
    return jax.shard_map(body, mesh=mesh, in_specs=in_specs, out_specs=out_specs, check_vma=False)
```

profile of v0, /device:TPU:0, one launch (start us, length us, event | category | flops | bytes accessed | tf_op | source)
XLA Modules:
  0.0 724.3 jit_solution(17834346506432816662)
XLA Ops:
  7.3 1.5 multiply_reduce_fusion.6
  8.8 2.2 multiply_convert_fusion.3
  14.7 45.1 %all-gather.5.cloned.1.call-done = bf16[1024,1024]{1,0:T(8,128)(2,1)} async-done(((bf16[256,1024]{1,0:T(8,128)(2,1)}), bf16[1024,1024]{1,0:T(8,128)(2,1)}) %all-gather.5.cloned.1.call-update) | async-done | bytes 2097168 | tf_op jit(solution)/shard_map/all_gather | solution.py:92
  59.8 3.1 fusion.74
  64.7 25.1 %while.28 = (s32[]{:T(128)}, bf16[2,512,2,2,64]{1,4,3,2,0:T(8,128)(2,1)}, f32[2,2,2,512]{3,2,1,0:T(2,128)}, s32[2]{0:T(128)S(1)}, s32[1024]{0:T(1024)S(1)}, /*in...) while((s32[]{:T(128)}, ...), condition=%wide.region_8.9_spmd.clone, body=%wide.region_5.8_spmd.clone.sunk | while | flops 563608064 | bytes 32979248 | solution.py:131
  68.6 1.9 bitcast_reduce_fusion.2
  70.5 2.4 fusion.130
  72.9 3.0 fusion.131
  81.2 1.9 bitcast_reduce_fusion.2
  83.1 2.4 fusion.130
  85.5 3.0 fusion.131
  89.9 1.6 copy.27
  92.4 2.8 fusion.75
  95.3 75.6 %reduce-scatter.5.cloned.1.call-done = f32[256,1024]{1,0:T(8,128)} async-done(((f32[1024,1024]{1,0:T(8,128)}), f32[256,1024]{1,0:T(8,128)}) %reduce-scatter.5.cloned.1.call-update) | async-done | bytes 1048592 | tf_op jit(solution)/shard_map/reduce_scatter | solution.py:133
  170.8 1.7 multiply_reduce_fusion.4
  174.6 2.1 convert_element_type.102
  176.9 44.2 %all-gather.7.cloned.1.call-done = bf16[1024,1024]{1,0:T(8,128)(2,1)} async-done(((bf16[256,1024]{1,0:T(8,128)(2,1)}), bf16[1024,1024]{1,0:T(8,128)(2,1)}) %all-gather.7.cloned.1.call-update) | async-done | bytes 2097168 | tf_op jit(solution)/shard_map/all_gather | solution.py:137
  221.1 7.5 %fusion.77 = f32[1024,1152]{1,0:T(8,128)} fusion(bf16[1024,1024]{1,0:T(8,128)(2,1)} %all-gather.7.cloned.1.call-done, bf16[1024,1152]{1,0:T(8,128)(2,1)} %param.30), kind=kOutput, calls=%fused_computation.151 | convolution fusion | flops 2415919104 | bytes 9175040 | tf_op jit(solution)/shard_map/dot_general | solution.py:47
  228.6 4.5 fusion.76
  233.1 35.0 %all-gather.9.cloned.1.call-done = bf16[1024,1024]{1,0:T(8,128)(2,1)} async-done(((bf16[256,1024]{1,0:T(8,128)(2,1)}), bf16[1024,1024]{1,0:T(8,128)(2,1)}) %all-gather.9.cloned.1.call-update) | async-done | bytes 2097168 | tf_op jit(solution)/shard_map/all_gather | solution.py:145
  268.1 9.3 %multiply_convert_fusion = (bf16[1024,1152]{1,0:T(8,128)(2,1)S(1)}, bf16[1024,1152]{1,0:T(8,128)(2,1)S(1)}, bf16[1024,1152]{1,0:T(8,128)(2,1)}) fusion(f32[1024,1152]{1,0:T(8,128)} %fusion.76, f32[1024,1152]{1,0:T(8,128)} %fusion.77, bf16[1024,1024]{1,0:T(8,128)(2,1)} %all-gather.9.cloned.1.call-done, bf16[1152,1024]{1,0:T(8,128)(2,1)S(1)} %copy-done), kind=kOutput, calls=%fused_computation.63 | convolution fusion | flops 2434793472 | bytes 20971520 | tf_op jit(solution)/shard_map/dot_general | solution.py:57
  277.5 2.9 fusion.78
  280.8 4.4 convolution_add_fusion
  285.3 5.8 convolution_convert_fusion.3
  291.2 69.5 %reduce-scatter.9.cloned.1.call-done = f32[256,1024]{1,0:T(8,128)} async-done(((f32[1024,1024]{1,0:T(8,128)}), f32[256,1024]{1,0:T(8,128)}) %reduce-scatter.9.cloned.1.call-update) | async-done | bytes 1048592 | tf_op jit(solution)/shard_map/reduce_scatter | solution.py:153
  360.7 1.6 multiply_reduce_fusion.1
  362.3 45.0 %reduce-scatter.7.cloned.1.call-done = bf16[256,1024]{1,0:T(8,128)(2,1)} async-done(((bf16[1024,1024]{1,0:T(8,128)(2,1)}), bf16[256,1024]{1,0:T(8,128)(2,1)}) %reduce-scatter.7.cloned.1.call-update) | async-done | bytes 524304 | tf_op jit(solution)/shard_map/reduce_scatter | solution.py:142
  407.3 3.2 fusion.71
  410.8 45.1 %all-gather.11.cloned.1.call-done = bf16[1024,1024]{1,0:T(8,128)(2,1)} async-done(((bf16[256,1024]{1,0:T(8,128)(2,1)}), bf16[1024,1024]{1,0:T(8,128)(2,1)}) %all-gather.11.cloned.1.call-update) | async-done | bytes 2097168 | tf_op jit(solution)/shard_map/all_gather | solution.py:161
  455.9 2.3 convolution_convert_fusion.7
  458.2 56.9 %while.29 = (s32[]{:T(128)}, f32[1024,2,64]{0,2,1:T(8,128)S(1)}, f32[1024,2,64]{0,2,1:T(8,128)}, f32[2,512,2,2,64]{1,0,4,3,2:T(2,128)}, s32[2]{0:T(128)S(1)}, /*...) while((s32[]{:T(128)}, f32[1024,2,64]{0,2,1:T(8,128)S(1)}, ...), condition=%wide.region_16.17_spmd.clone, body=%wide.region_14.16_spmd.clone.sunk | while | flops 1375992320 | bytes 71637232 | solution.py:200
  462.1 1.4 fusion.140
  463.5 3.3 fusion.145
  466.8 3.5 fusion.142
  470.3 2.4 fusion.143
  473.7 1.4 fusion.146
  475.6 10.4 %dynamic_update_slice.21 = f32[2,512,2,2,64]{1,0,4,3,2:T(2,128)} dynamic-update-slice(f32[2,512,2,2,64]{1,0,4,3,2:T(2,128)} %get-tuple-element.474, f32[1,512,2,2,64]{1,0,4,3,2:T(1,128)S(1)} %copy.55, s32[]{:T(128)S(6)} %copy.74, s32[]{:T(128)} %constant.46.clone.1..sunk.1, s32[]{:T(128)} %constant.46.clone.1..sunk.1, s32[]{:T(128)} %constant.46.clone.1..sunk.1, s32[]{:T(128)} %constant.46.clone.1..sunk.1) | dynamic-update-slice | bytes 1048580 | tf_op jit(solution)/shard_map/while/body/jit(dynamic_update_index_in_dim)/dynamic_update_slice | solution.py:131
  489.9 1.4 fusion.140
  491.3 4.4 fusion.145
  495.6 3.5 fusion.142
  499.1 2.4 fusion.143
  501.6 1.0 fusion.144
  502.5 1.4 fusion.146
  504.5 10.4 %dynamic_update_slice.21 = f32[2,512,2,2,64]{1,0,4,3,2:T(2,128)} dynamic-update-slice(f32[2,512,2,2,64]{1,0,4,3,2:T(2,128)} %get-tuple-element.474, f32[1,512,2,2,64]{1,0,4,3,2:T(1,128)S(1)} %copy.55, s32[]{:T(128)S(6)} %copy.74, s32[]{:T(128)} %constant.46.clone.1..sunk.1, s32[]{:T(128)} %constant.46.clone.1..sunk.1, s32[]{:T(128)} %constant.46.clone.1..sunk.1, s32[]{:T(128)} %constant.46.clone.1..sunk.1) | dynamic-update-slice | bytes 1048580 | tf_op jit(solution)/shard_map/while/body/jit(dynamic_update_index_in_dim)/dynamic_update_slice | solution.py:131
  515.1 3.1 reshape.270
  518.3 1.6 multiply_add_fusion.1
  521.9 1.1 convert.36
  523.0 2.6 convolution_convert_fusion.4
  525.7 6.5 convolution_convert_fusion
  532.2 4.2 convolution_convert_fusion.1
  536.5 4.2 convolution_convert_fusion.2
  540.7 1.5 convolution_convert_fusion.6
  542.3 2.3 convolution_convert_fusion.5
  544.6 23.7 %reduce-scatter.11.cloned.1.call-done = bf16[256,1024]{1,0:T(8,128)(2,1)} async-done(((bf16[1024,1024]{1,0:T(8,128)(2,1)}), bf16[256,1024]{1,0:T(8,128)(2,1)}) %reduce-scatter.11.cloned.1.call-update) | async-done | bytes 524304 | tf_op jit(solution)/shard_map/reduce_scatter | solution.py:214
  568.4 1.4 fusion.58
  569.8 40.4 %all-reduce.4 = (f32[1024]{0:T(1024)}, f32[1024]{0:T(1024)}, f32[64]{0:T(128)}, f32[64]{0:T(128)}) all-reduce(f32[1024]{0:T(1024)S(1)} %get-tuple-element.203, f32[1024]{0:T(1024)S(1)} %get-tuple-element.201, f32[64]{0:T(128)S(1)} %get-tuple-element.205, f32[64]{0:T(128)S(1)} %get-tuple-element.207), channel_id=1, replica_groups=mesh['dp'=8,'mp'=4] {'dp','mp'}, use_global_device_ids=true, to_apply=%region_22.23 | all-reduce | flops 2176 | bytes 17408 | tf_op jit(solution)/shard_map/psum | solution.py:219
  610.2 2.3 fusion.61
  612.5 92.5 %all-reduce.8.cloned.1.call-done = (bf16[1024,512]{1,0:T(8,128)(2,1)}, bf16[256,1024]{1,0:T(8,128)(2,1)}, bf16[1024,1152]{1,0:T(8,128)(2,1)}, bf16[1024,1152]{1,0:T(8,128)(2,1)}, bf16[1152,1024]{1,0:T(8,128)(2,1)}) async-done(((bf16[1024,512]{1,0:T(8,128)(2,1)}, bf16[256,1024]{1,0:T(8,128)(2,1)}, bf16[1024,1152]{1,0:T(8,128)(2,1)}, bf16[1024,1152]{1,0:T(8,128)(2,1)}, bf16[1152,1024]{1,0:T(8,128)(2,1)}), ...) | async-done | bytes 8650768 | tf_op jit(solution)/shard_map/psum | solution.py:221
  705.0 2.2 slice.71
  707.2 1.0 fusion.73
  708.2 1.1 convert_element_type.112
  709.3 2.5 convert_element_type.114
  711.9 2.5 convert_element_type.116
  714.6 2.7 convert_element_type.118
  (219 shorter events, 23.5 us)
Async XLA Ops:
  7.2 260.9 %copy-start = (bf16[1152,1024]{1,0:T(8,128)(2,1)S(1)}, bf16[1152,1024]{1,0:T(8,128)(2,1)}, u32[]{:S(2)}) copy-start(bf16[1152,1024]{1,0:T(8,128)(2,1)} %param.31) | copy-start | bytes 7077892
  7.2 3.9 copy-start.19
  7.2 5.7 copy-start.23
  7.2 5.7 copy-start.30
  7.2 5.8 copy-start.31
  7.2 52.6 %all-gather.5.cloned.1.call-start = ((), (), s32[]{:S(2)}) async-start(), calls=%async_computation.4 | async-start | bytes 2621440 | tf_op jit(solution)/shard_map/all_gather | solution.py:92
  8.8 3.5 copy-start.45
  8.8 3.5 copy-start.43
  11.0 159.8 %reduce-scatter.5.cloned.1.call-start = ((), (), s32[]{:S(2)}) async-start(), calls=%async_computation.5 | async-start | bytes 5242880 | tf_op jit(solution)/shard_map/reduce_scatter | solution.py:133
  14.7 49.8 %copy-start.12 = (f32[1024,32]{0,1:T(8,128)}, f32[1024,32]{0,1:T(8,128)S(1)}, u32[]{:S(2)}) copy-start(f32[1024,32]{0,1:T(8,128)S(1)} %get-tuple-element.282) | copy-start | bytes 393220
  14.7 49.8 %copy-start.14 = (f32[1024,32]{0,1:T(8,128)}, f32[1024,32]{0,1:T(8,128)S(1)}, u32[]{:S(2)}) copy-start(f32[1024,32]{0,1:T(8,128)S(1)} %get-tuple-element.283) | copy-start | bytes 393220
  14.7 49.1 %copy-start.47 = (f32[64]{0:T(128)S(1)}, f32[64]{0:T(128)}, u32[]{:S(2)}) copy-start(f32[64]{0:T(128)} %param.24) | copy-start | bytes 772
  63.0 1.4 copy-start.2
  63.2 1.2 copy-start.32
  70.5 2.4 copy-start.24
  72.9 3.0 copy-start.36
  83.1 2.4 copy-start.24
  85.5 3.0 copy-start.36
  89.9 2.5 copy-start.20
  95.2 78.3 %copy-start.41 = (f32[1024]{0:T(1024)S(1)}, f32[1024]{0:T(1024)}, u32[]{:S(2)}) copy-start(f32[1024]{0:T(1024)} %param.22) | copy-start | bytes 12292
  95.2 125.9 %all-gather.7.cloned.1.call-start = ((), (), s32[]{:S(2)}) async-start(), calls=%async_computation.6 | async-start | bytes 2621440 | tf_op jit(solution)/shard_map/all_gather | solution.py:137
  174.5 93.6 %all-gather.9.cloned.1.call-start = ((), (), s32[]{:S(2)}) async-start(), calls=%async_computation.8 | async-start | bytes 2621440 | tf_op jit(solution)/shard_map/all_gather | solution.py:145
  176.7 184.0 %reduce-scatter.9.cloned.1.call-start = ((), (), s32[]{:S(2)}) async-start(), calls=%async_computation.9 | async-start | bytes 5242880 | tf_op jit(solution)/shard_map/reduce_scatter | solution.py:153
  221.1 7.5 %copy-start.51 = (bf16[1024,1152]{1,0:T(8,128)(2,1)S(1)}, bf16[1024,1152]{1,0:T(8,128)(2,1)}, u32[]{:S(2)}) copy-start(bf16[1024,1152]{1,0:T(8,128)(2,1)} %param.29) | copy-start | bytes 7077892
  221.1 7.5 %copy-start.55 = (bf16[1024,1024]{1,0:T(8,128)(2,1)S(1)}, bf16[1024,1024]{1,0:T(8,128)(2,1)}, u32[]{:S(2)}) copy-start(bf16[1024,1024]{1,0:T(8,128)(2,1)} %all-gather.7.cloned.1.call-done) | copy-start | bytes 6291460
  268.1 9.3 %copy-start.52 = (bf16[1024,1152]{1,0:T(8,128)(2,1)S(1)}, bf16[1024,1152]{1,0:T(8,128)(2,1)}, u32[]{:S(2)}) copy-start(bf16[1024,1152]{1,0:T(8,128)(2,1)} %param.29) | copy-start | bytes 7077892
  277.4 2.9 copy-start.60
  277.5 2.9 copy-start.58
  277.5 3.4 copy-start.53
  285.3 122.0 %reduce-scatter.7.cloned.1.call-start = ((), (), s32[]{:S(2)}) async-start(), calls=%async_computation.7 | async-start | bytes 2621440 | tf_op jit(solution)/shard_map/reduce_scatter | solution.py:142
  291.1 69.6 %copy-start.6 = (f32[256,1024]{1,0:T(8,128)S(1)}, f32[256,1024]{1,0:T(8,128)}, u32[]{:S(2)}) copy-start(f32[256,1024]{1,0:T(8,128)} %copy-done.5) | copy-start | bytes 3145732
  291.2 164.7 %all-gather.11.cloned.1.call-start = ((), (), s32[]{:S(2)}) async-start(), calls=%async_computation.10 | async-start | bytes 2621440 | tf_op jit(solution)/shard_map/all_gather | solution.py:161
  360.7 46.6 %copy-start.7 = (f32[256,1024]{1,0:T(8,128)S(1)}, f32[256,1024]{1,0:T(8,128)}, u32[]{:S(2)}) copy-start(f32[256,1024]{1,0:T(8,128)} %reduce-scatter.9.cloned.1.call-done) | copy-start | bytes 3145732
  410.4 45.4 %copy-start.21 = (bf16[256,1024]{1,0:T(8,128)(2,1)S(1)}, bf16[256,1024]{1,0:T(8,128)(2,1)}, u32[]{:S(2)}) copy-start(bf16[256,1024]{1,0:T(8,128)(2,1)} %param.28) | copy-start | bytes 1572868
  410.5 157.9 %reduce-scatter.11.cloned.1.call-start = ((), (), s32[]{:S(2)}) async-start(), calls=%async_computation.11 | async-start | bytes 2621440 | tf_op jit(solution)/shard_map/reduce_scatter | solution.py:214
  410.8 47.5 %copy-start.38 = (f32[2,2,2,512]{3,2,1,0:T(2,128)S(1)}, f32[2,2,2,512]{3,2,1,0:T(2,128)}, u32[]{:S(2)}) copy-start(f32[2,2,2,512]{3,2,1,0:T(2,128)} %get-tuple-element.465) | copy-start | bytes 49156
  458.2 60.0 %copy-start.13 = (f32[1024,32]{0,1:T(8,128)S(1)}, f32[1024,32]{0,1:T(8,128)}, u32[]{:S(2)}) copy-start(f32[1024,32]{0,1:T(8,128)} %copy-done.12) | copy-start | bytes 393220
  515.1 4.7 copy-start.15
  518.3 1.9 copy-start.3
  518.3 2.2 slice-start.1
  518.3 2.2 copy-start.27
  518.3 2.2 copy-start.50
  519.8 1.1 copy-start.33
  520.5 1.0 slice-start
  520.5 1.0 copy-start.35
  521.2 1.8 copy-start.29
  525.6 179.3 %all-reduce.8.cloned.1.call-start = ((), (), s32[]{:S(2)}) async-start(), calls=%async_computation.12 | async-start | bytes 17301504 | tf_op jit(solution)/shard_map/psum | solution.py:221
  525.7 6.5 copy-start.56
  525.7 6.5 copy-start.59
  532.2 4.2 copy-start.61
  536.5 4.2 copy-start.11
  536.5 4.2 copy-start.57
  540.7 1.6 copy-start.54
  544.6 23.8 %copy-start.4 = (f32[256,1024]{1,0:T(8,128)S(1)}, f32[256,1024]{1,0:T(8,128)}, u32[]{:S(2)}) copy-start(f32[256,1024]{1,0:T(8,128)} %param.18) | copy-start | bytes 3145732
  544.6 23.8 %copy-start.42 = (f32[1024]{0:T(1024)S(1)}, f32[1024]{0:T(1024)}, u32[]{:S(2)}) copy-start(f32[1024]{0:T(1024)} %param.21) | copy-start | bytes 12292
  544.6 23.8 %copy-start.44 = (f32[256]{0:T(256)S(1)}, f32[256]{0:T(256)}, u32[]{:S(2)}) copy-start(f32[256]{0:T(256)} %copy-done.43) | copy-start | bytes 3076
  544.6 65.5 %copy-start.46 = (f32[256]{0:T(256)S(1)}, f32[256]{0:T(256)}, u32[]{:S(2)}) copy-start(f32[256]{0:T(256)} %copy-done.45) | copy-start | bytes 3076
  544.6 65.6 %copy-start.8 = (f32[256,1024]{1,0:T(8,128)S(1)}, f32[256,1024]{1,0:T(8,128)}, u32[]{:S(2)}) copy-start(f32[256,1024]{1,0:T(8,128)} %get-tuple-element.261) | copy-start | bytes 3145732
  705.0 2.2 copy-start.9
  705.0 3.2 copy-start.22
  707.2 2.1 copy-start.18
  709.3 2.6 copy-start.17
  711.9 2.6 copy-start.16
  714.4 2.9 copy-start.1
  (13 other events, 10.2 us)
Sparse Core Ops, SparseCore 0:
  11.2 48.6 all-gather.4
  95.3 75.4 reduce-scatter.4
  174.6 46.4 all-gather.6
  223.2 44.8 all-gather.8
  285.4 75.2 reduce-scatter.8
  362.8 44.3 reduce-scatter.6
  410.6 45.2 all-gather.10
  525.8 42.5 reduce-scatter.10
  573.9 131.0 all-reduce.7
where the time goes:
time: 734 us; the launch traced here: 724 us
  waiting for transfers between devices  476 us (65%)
  matrix products  96 us (13%)
  other arithmetic  45.9 us (6%)
  local copies, waits for them, and re-layouts  41.5 us (6%)
  blocking collectives  40.4 us (6%)
  between operations  15.6 us (2%)
  loops' own time  8.26 us (1%)
    psum x1, waiting for transfers between devices, body(): lax.psum(joined_wgrad.astype(jnp.bfloat16), 'dp').astype(jnp.float32)  92.5 us
    reduce_scatter x1, waiting for transfers between devices, body(): lax.psum_scatter(dot_plain(attended, o_weight), 'mp', scatter_dimension=0...  75.6 us
    reduce_scatter x1, waiting for transfers between devices, body(): lax.psum_scatter(dot_right_t(grad_gate, gate_weight) + dot_right_t(grad_u...  69.5 us
    all_gather x1, waiting for transfers between devices, body(): lax.all_gather(grad_mid.astype(jnp.bfloat16), 'mp', axis=0, tiled=True)  45.1 us
    all_gather x1, waiting for transfers between devices, body(): lax.all_gather(normed_one.astype(jnp.bfloat16), 'mp', axis=0, tiled=True)  45.1 us
    reduce_scatter x1, waiting for transfers between devices, body(): lax.psum_scatter(dot_plain(act_low, down_weight).astype(jnp.bfloat16), 'm...  45 us
    all_gather x1, waiting for transfers between devices, body(): lax.all_gather(normed_two.astype(jnp.bfloat16), 'mp', axis=0, tiled=True)  44.2 us
    psum x1, blocking collectives, body(): lax.psum((gain1_grad, gain2_grad, qgain_grad, kgain_grad), ('dp', 'mp'))  40.4 us
  transfers between devices with their start and end apart: 9, of which 9 were waited for; matrix products, arithmetic and copies ran while one was open for 6% of the time, Pallas kernels for 0%

commit v1 on v0

--- a/solution.py
+++ b/solution.py
@@ -91,6 +91,8 @@
     normed_one, norm1_back = jax.vjp(normed, inputs, norm1_gain)
     hidden = lax.all_gather(normed_one.astype(jnp.bfloat16), "mp", axis=0, tiled=True)
     joined = jnp.concatenate([q_weight, k_weight, v_weight], 1)
+    hidden, cotangent_low = lax.optimization_barrier((hidden, cotangent.astype(jnp.bfloat16)))
+    grad_full = lax.all_gather(cotangent_low, "mp", axis=0, tiled=True)
     projected = dot_plain(hidden, joined)
     query_raw = projected[:, :query_cols].reshape(full_len, query_heads, HEAD)
     key_raw = projected[:, query_cols : query_cols + key_cols].reshape(full_len, kv_heads, HEAD)
@@ -131,8 +133,8 @@
     block_out, log_totals = lax.map(forward_block, block_starts)
     attended = block_out.reshape(full_len, query_cols).astype(jnp.bfloat16)
     mid_rows = inputs + lax.psum_scatter(
-        dot_plain(attended, o_weight), "mp", scatter_dimension=0, tiled=True
-    )
+        dot_plain(attended, o_weight).astype(jnp.bfloat16), "mp", scatter_dimension=0, tiled=True
+    ).astype(jnp.float32)
     normed_two, norm2_back = jax.vjp(normed, mid_rows, norm2_gain)
     hidden_mid = lax.all_gather(normed_two.astype(jnp.bfloat16), "mp", axis=0, tiled=True)
     gate_pre = dot_plain(hidden_mid, gate_weight)
@@ -142,7 +144,6 @@
     result = mid_rows + lax.psum_scatter(
         dot_plain(act_low, down_weight).astype(jnp.bfloat16), "mp", scatter_dimension=0, tiled=True
     ).astype(jnp.float32)
-    grad_full = lax.all_gather(cotangent.astype(jnp.bfloat16), "mp", axis=0, tiled=True)
     grad_act = dot_right_t(grad_full, down_weight)
     down_wgrad = dot_left_t(act_low, grad_full)
     grad_gate, grad_up = gated_back(grad_act)
@@ -151,10 +152,18 @@
     gate_wgrad = dot_left_t(hidden_mid, grad_gate)
     up_wgrad = dot_left_t(hidden_mid, grad_up)
     grad_normed_mid = lax.psum_scatter(
-        dot_right_t(grad_gate, gate_weight) + dot_right_t(grad_up, up_weight),
+        (dot_right_t(grad_gate, gate_weight) + dot_right_t(grad_up, up_weight)).astype(jnp.bfloat16),
         "mp",
         scatter_dimension=0,
         tiled=True,
+    ).astype(jnp.float32)
+    down_total, gate_total, up_total = lax.psum(
+        (
+            down_wgrad.astype(jnp.bfloat16),
+            gate_wgrad.astype(jnp.bfloat16),
+            up_wgrad.astype(jnp.bfloat16),
+        ),
+        "dp",
     )
     grad_mid_norm, gain2_grad = norm2_back(grad_normed_mid)
     grad_mid = cotangent + grad_mid_norm
@@ -216,14 +225,24 @@
     ).astype(jnp.float32)
     grad_in_norm, gain1_grad = norm1_back(grad_normed_in)
     inputs_grad = grad_mid + grad_in_norm
-    gain_totals = lax.psum((gain1_grad, gain2_grad, qgain_grad, kgain_grad), ("dp", "mp"))
-    joined_wgrad, out_wgrad, gate_wgrad, up_wgrad, down_wgrad = (
-        lax.psum(joined_wgrad.astype(jnp.bfloat16), "dp").astype(jnp.float32),
-        lax.psum(out_wgrad.astype(jnp.bfloat16), "dp").astype(jnp.float32),
-        lax.psum(gate_wgrad.astype(jnp.bfloat16), "dp").astype(jnp.float32),
-        lax.psum(up_wgrad.astype(jnp.bfloat16), "dp").astype(jnp.float32),
-        lax.psum(down_wgrad.astype(jnp.bfloat16), "dp").astype(jnp.float32),
-    )
+    gains = jnp.concatenate([gain1_grad, gain2_grad, qgain_grad, kgain_grad])
+    gains = jnp.sum(lax.all_gather(gains, ("dp", "mp"), axis=0), 0)
+    width = gain1_grad.shape[0]
+    gain_totals = (
+        gains[:width],
+        gains[width : 2 * width],
+        gains[2 * width : 2 * width + HEAD],
+        gains[2 * width + HEAD :],
+    )
+    joined_low, out_low, down_total = lax.optimization_barrier(
+        (joined_wgrad.astype(jnp.bfloat16), out_wgrad.astype(jnp.bfloat16), down_total)
+    )
+    joined_wgrad, out_wgrad = lax.psum((joined_low, out_low), "dp")
+    joined_wgrad = joined_wgrad.astype(jnp.float32)
+    out_wgrad = out_wgrad.astype(jnp.float32)
+    gate_wgrad = gate_total.astype(jnp.float32)
+    up_wgrad = up_total.astype(jnp.float32)
+    down_wgrad = down_total.astype(jnp.float32)
     query_wgrad = joined_wgrad[:, :query_cols]
     key_wgrad = joined_wgrad[:, query_cols : query_cols + key_cols]
     value_wgrad = joined_wgrad[:, query_cols + key_cols :]

time: 734 us -> 675 us (0.920)
  waiting for transfers between devices: 476 us -> 358 us
  blocking collectives: 40.4 us -> 76.6 us
  local copies, waits for them, and re-layouts: 41.5 us -> 49.9 us
  matrix products: 96 us -> 104 us
    all_gather x0 -> x1, blocking collectives: none -> 76.6 us  [body(): gains = jnp.sum(lax.all_gather(gains, ('dp', 'mp'), axis=0), 0)]
    reduce_scatter x2, waiting for transfers between devices: 145 us -> 85.8 us  [the longest x1 43 us: body(): lax.psum_scatter(dot_plain(attended, o_weight).astype(jnp.bfloat16), 'mp'...]
    reduce_scatter x1, waiting for transfers between devices: 45 us -> 0.01 us  [body(): lax.psum_scatter(dot_plain(act_low, down_weight).astype(jnp.bfloat16), 'm...]
    psum x1 -> x0, blocking collectives: 40.4 us -> none  [body(): lax.psum((gain1_grad, gain2_grad, qgain_grad, kgain_grad), ('dp', 'mp'))]
    all_gather x1, waiting for transfers between devices: 45.1 us -> 26.9 us  [body(): lax.all_gather(grad_mid.astype(jnp.bfloat16), 'mp', axis=0, tiled=True)]
    reduce_scatter x1, waiting for transfers between devices: 23.7 us -> 35.7 us  [body(): lax.psum_scatter(dot_right_t(grad_joined, joined).astype(jnp.bfloat16), '...]
    psum x1 -> x2, waiting for transfers between devices: 92.5 us -> 88.7 us  [the longest x1 88.7 us: body(): joined_wgrad, out_wgrad = lax.psum((joined_low, out_low), 'dp')]
  transfers between devices with their start and end apart: 9 -> 10, of which waited for: 9 -> 8; matrix products, arithmetic and copies ran while one was open for 6% -> 20% of each run, Pallas kernels for 0% -> 0%
where the time goes in v1:
time: 675 us; the launch traced here: 665 us
  waiting for transfers between devices  358 us (53%)
  matrix products  104 us (15%)
  blocking collectives  76.6 us (11%)
  other arithmetic  51.2 us (8%)
  local copies, waits for them, and re-layouts  49.9 us (7%)
  between operations  16 us (2%)
  loops' own time  8.56 us (1%)
    psum x1, waiting for transfers between devices, body(): joined_wgrad, out_wgrad = lax.psum((joined_low, out_low), 'dp')  88.7 us
    all_gather x1, blocking collectives, body(): gains = jnp.sum(lax.all_gather(gains, ('dp', 'mp'), axis=0), 0)  76.6 us
    all_gather x1, waiting for transfers between devices, body(): lax.all_gather(normed_two.astype(jnp.bfloat16), 'mp', axis=0, tiled=True)  44.6 us
    reduce_scatter x1, waiting for transfers between devices, body(): lax.psum_scatter(dot_plain(attended, o_weight).astype(jnp.bfloat16), 'mp'...  43 us
    reduce_scatter x1, waiting for transfers between devices, body(): lax.psum_scatter((dot_right_t(grad_gate, gate_weight) + dot_right_t(grad_...  42.9 us
    all_gather x1, waiting for transfers between devices, body(): lax.all_gather(normed_one.astype(jnp.bfloat16), 'mp', axis=0, tiled=True)  41.1 us
    reduce_scatter x1, waiting for transfers between devices, body(): lax.psum_scatter(dot_right_t(grad_joined, joined).astype(jnp.bfloat16), '...  35.7 us
    all_gather x1, waiting for transfers between devices, body(): grad_full = lax.all_gather(cotangent_low, 'mp', axis=0, tiled=True)  35 us
  transfers between devices with their start and end apart: 10, of which 8 were waited for; matrix products, arithmetic and copies ran while one was open for 20% of the time, Pallas kernels for 0%

profile of v1, /device:TPU:0, one launch (start us, length us, event | category | flops | bytes accessed | tf_op | source)
XLA Modules:
  0.0 665.0 jit_solution(744669629453944882)
XLA Ops:
  7.3 1.5 multiply_reduce_fusion.4
  9.9 2.2 multiply_convert_fusion.3
  19.6 41.1 %all-gather.7.cloned.1.call-done = bf16[1024,1024]{1,0:T(8,128)(2,1)} async-done(((bf16[256,1024]{1,0:T(8,128)(2,1)}), bf16[1024,1024]{1,0:T(8,128)(2,1)}) %all-gather.7.cloned.1.call-update) | async-done | bytes 2097168 | tf_op jit(solution)/shard_map/all_gather | solution.py:92
  60.7 3.1 fusion.79
  67.2 25.8 %while.28 = (s32[]{:T(128)}, bf16[2,512,2,2,64]{1,4,3,2,0:T(8,128)(2,1)}, f32[2,2,2,512]{3,2,1,0:T(2,128)S(1)}, s32[2]{0:T(128)S(1)}, s32[1024]{0:T(1024)S(1)}, ...) while((s32[]{:T(128)}, ...), condition=%wide.region_8.9_spmd.clone, body=%wide.region_5.8_spmd.clone.sunk | while | flops 563608064 | bytes 32848120 | solution.py:133
  71.1 2.9 bitcast_reduce_fusion.2
  73.9 2.4 fusion.134
  76.3 3.0 fusion.135
  84.0 2.8 bitcast_reduce_fusion.2
  86.8 2.4 fusion.134
  89.2 3.0 fusion.135
  93.0 1.8 copy.29
  95.7 2.1 convolution_convert_fusion.5
  97.8 43.0 %reduce-scatter.5.cloned.1.call-done = bf16[256,1024]{1,0:T(8,128)(2,1)} async-done(((bf16[1024,1024]{1,0:T(8,128)(2,1)}), bf16[256,1024]{1,0:T(8,128)(2,1)}) %reduce-scatter.5.cloned.1.call-update) | async-done | bytes 524304 | tf_op jit(solution)/shard_map/reduce_scatter | solution.py:135
  140.8 1.3 multiply_reduce_fusion.2
  142.1 2.0 multiply_convert_fusion.2
  144.9 44.6 %all-gather.9.cloned.1.call-done = bf16[1024,1024]{1,0:T(8,128)(2,1)} async-done(((bf16[256,1024]{1,0:T(8,128)(2,1)}), bf16[1024,1024]{1,0:T(8,128)(2,1)}) %all-gather.9.cloned.1.call-update) | async-done | bytes 2097168 | tf_op jit(solution)/shard_map/all_gather | solution.py:139
  189.6 7.5 %fusion.81 = f32[1024,1152]{1,0:T(8,128)} fusion(bf16[1024,1024]{1,0:T(8,128)(2,1)} %all-gather.9.cloned.1.call-done, bf16[1024,1152]{1,0:T(8,128)(2,1)} %param.30), kind=kOutput, calls=%fused_computation.158 | convolution fusion | flops 2415919104 | bytes 9175040 | tf_op jit(solution)/shard_map/dot_general | solution.py:47
  197.1 4.5 fusion.80
  201.5 35.0 %all-gather.11.cloned.1.call-done = bf16[1024,1024]{1,0:T(8,128)(2,1)} async-done(((bf16[256,1024]{1,0:T(8,128)(2,1)}), bf16[1024,1024]{1,0:T(8,128)(2,1)}) %all-gather.11.cloned.1.call-update) | async-done | bytes 2097168 | tf_op jit(solution)/shard_map/all_gather | solution.py:95
  236.5 9.3 %multiply_convert_fusion = (bf16[1024,1152]{1,0:T(8,128)(2,1)S(1)}, bf16[1024,1152]{1,0:T(8,128)(2,1)S(1)}, bf16[1024,1152]{1,0:T(8,128)(2,1)}) fusion(f32[1024,1152]{1,0:T(8,128)} %fusion.80, f32[1024,1152]{1,0:T(8,128)} %fusion.81, bf16[1024,1024]{1,0:T(8,128)(2,1)} %all-gather.11.cloned.1.call-done, bf16[1152,1024]{1,0:T(8,128)(2,1)S(1)} %copy-done), kind=kOutput, calls=%fused_computation.63 | convolution fusion | flops 2434793472 | bytes 20971520 | tf_op jit(solution)/shard_map/dot_general | solution.py:57
  245.9 2.9 fusion.82
  249.3 4.1 add_convert_fusion
  253.5 42.9 %reduce-scatter.9.cloned.1.call-done = bf16[256,1024]{1,0:T(8,128)(2,1)} async-done(((bf16[1024,1024]{1,0:T(8,128)(2,1)}), bf16[256,1024]{1,0:T(8,128)(2,1)}) %reduce-scatter.9.cloned.1.call-update) | async-done | bytes 524304 | tf_op jit(solution)/shard_map/reduce_scatter | solution.py:154
  296.3 2.4 fusion.61
  298.7 1.2 fusion.75
  300.0 1.6 copy-done.65
  301.6 5.6 convolution_convert_fusion.2
  307.3 6.9 %convolution_convert_fusion = bf16[1024,1152]{1,0:T(8,128)(2,1)} fusion(bf16[1024,1024]{1,0:T(8,128)(2,1)} %all-gather.9.cloned.1.call-done, bf16[1024,1152]{1,0:T(8,128)(2,1)} %copy-done.68), kind=kOutput, calls=%fused_computation.68 | convolution fusion | flops 2417098752 | bytes 6815744 | tf_op jit(solution)/shard_map/dot_general | solution.py:51
  314.3 4.2 convolution_convert_fusion.1
  318.5 26.9 %all-gather.13.cloned.1.call-done = bf16[1024,1024]{1,0:T(8,128)(2,1)} async-done(((bf16[256,1024]{1,0:T(8,128)(2,1)}), bf16[1024,1024]{1,0:T(8,128)(2,1)}) %all-gather.13.cloned.1.call-update) | async-done | bytes 2097168 | tf_op jit(solution)/shard_map/all_gather | solution.py:170
  345.3 3.2 convolution_convert_fusion.8
  348.6 62.4 %while.29 = (s32[]{:T(128)}, f32[1024,2,64]{0,2,1:T(8,128)}, f32[1024,2,64]{0,2,1:T(8,128)}, f32[2,512,2,2,64]{1,0,4,3,2:T(2,128)}, s32[2]{0:T(128)S(1)}, /*inde...) while((s32[]{:T(128)}, f32[1024,2,64]{0,2,1:T(8,128)}, ...), condition=%wide.region_16.17_spmd.clone, body=%wide.region_14.16_spmd.clone.sunk | while | flops 1375992320 | bytes 82123168 | solution.py:209
  353.3 2.5 fusion.144
  355.9 3.3 fusion.149
  359.2 3.5 fusion.146
  362.7 2.4 fusion.147
  366.1 1.4 fusion.150
  367.5 1.3 copy.58
  368.8 10.4 %dynamic_update_slice.21 = f32[2,512,2,2,64]{1,0,4,3,2:T(2,128)} dynamic-update-slice(f32[2,512,2,2,64]{1,0,4,3,2:T(2,128)} %get-tuple-element.480, f32[1,512,2,2,64]{1,0,4,3,2:T(1,128)} %copy.58, s32[]{:T(128)S(6)} %copy.77, s32[]{:T(128)} %constant.46.clone.1..sunk.1, s32[]{:T(128)} %constant.46.clone.1..sunk.1, s32[]{:T(128)} %constant.46.clone.1..sunk.1, s32[]{:T(128)} %constant.46.clone.1..sunk.1) | dynamic-update-slice | bytes 1048580 | tf_op jit(solution)/shard_map/while/body/jit(dynamic_update_index_in_dim)/dynamic_update_slice | solution.py:133
  383.8 2.5 fusion.144
  386.3 4.4 fusion.149
  390.7 3.5 fusion.146
  394.2 2.4 fusion.147
  397.6 1.4 fusion.150
  399.0 1.3 copy.58
  400.3 10.4 %dynamic_update_slice.21 = f32[2,512,2,2,64]{1,0,4,3,2:T(2,128)} dynamic-update-slice(f32[2,512,2,2,64]{1,0,4,3,2:T(2,128)} %get-tuple-element.480, f32[1,512,2,2,64]{1,0,4,3,2:T(1,128)} %copy.58, s32[]{:T(128)S(6)} %copy.77, s32[]{:T(128)} %constant.46.clone.1..sunk.1, s32[]{:T(128)} %constant.46.clone.1..sunk.1, s32[]{:T(128)} %constant.46.clone.1..sunk.1, s32[]{:T(128)} %constant.46.clone.1..sunk.1) | dynamic-update-slice | bytes 1048580 | tf_op jit(solution)/shard_map/while/body/jit(dynamic_update_index_in_dim)/dynamic_update_slice | solution.py:133
  411.0 3.1 reshape.270
  414.1 1.5 multiply_add_fusion.1
  417.6 1.2 convert.36
  419.5 1.5 convolution_convert_fusion.7
  421.4 2.3 convolution_convert_fusion.6
  423.8 4.2 convolution_convert_fusion.4
  428.1 6.1 convolution_convert_fusion.3
  434.2 4.4 convert_element_type.134
  438.6 88.7 %all-reduce.10.cloned.1.call-done = (bf16[1024,512]{1,0:T(8,128)(2,1)}, bf16[256,1024]{1,0:T(8,128)(2,1)}, bf16[1024,1152]{1,0:T(8,128)(2,1)}, bf16[1024,1152]{1,0:T(8,128)(2,1)}) async-done(((bf16[1024,512]{1,0:T(8,128)(2,1)}, bf16[256,1024]{1,0:T(8,128)(2,1)}, bf16[1024,1152]{1,0:T(8,128)(2,1)}, bf16[1024,1152]{1,0:T(8,128)(2,1)}), (bf16[1024,512]{1,0:T(8,128)(2,1)}, bf16[256,1024]{1,0:T(8,128)(2,1)}, ...) | async-done | bytes 6291472 | tf_op jit(solution)/shard_map/psum | solution.py:240
  527.3 2.3 convert_element_type.129
  529.6 2.1 slice.91
  531.7 2.5 convert_element_type.131
  534.3 2.5 convert_element_type.133
  537.9 35.7 %reduce-scatter.11.cloned.1.call-done = bf16[256,1024]{1,0:T(8,128)(2,1)} async-done(((bf16[1024,1024]{1,0:T(8,128)(2,1)}), bf16[256,1024]{1,0:T(8,128)(2,1)}) %reduce-scatter.11.cloned.1.call-update) | async-done | bytes 524304 | tf_op jit(solution)/shard_map/reduce_scatter | solution.py:223
  573.6 1.4 fusion.62
  575.1 76.6 %all-gather.1 = f32[32,1,2176]{2,1,0:T(1,128)} all-gather(f32[1,1,2176]{2,1,0:T(1,128)S(1)} %reshape.275), channel_id=2, replica_groups=mesh['dp'=8,'mp'=4] {'dp','mp'}, dimensions={0}, use_global_device_ids=true | all-gather | bytes 287232 | tf_op jit(solution)/shard_map/all_gather | solution.py:229
  654.0 3.8 fusion.65
  (249 shorter events, 32.7 us)
Async XLA Ops:
  7.2 229.4 %copy-start = (bf16[1152,1024]{1,0:T(8,128)(2,1)S(1)}, bf16[1152,1024]{1,0:T(8,128)(2,1)}, u32[]{:S(2)}) copy-start(bf16[1152,1024]{1,0:T(8,128)(2,1)} %param.31) | copy-start | bytes 7077892
  7.2 5.0 copy-start.25
  7.2 6.6 copy-start.13
  7.2 53.5 %all-gather.7.cloned.1.call-start = ((), (), s32[]{:S(2)}) async-start(), calls=%async_computation.4 | async-start | bytes 2621440 | tf_op jit(solution)/shard_map/all_gather | solution.py:92
  12.1 128.7 %reduce-scatter.5.cloned.1.call-start = ((), (), s32[]{:S(2)}) async-start(), calls=%async_computation.5 | async-start | bytes 2621440 | tf_op jit(solution)/shard_map/reduce_scatter | solution.py:135
  19.6 46.6 %copy-start.18 = (f32[1024,32]{0,1:T(8,128)}, f32[1024,32]{0,1:T(8,128)S(1)}, u32[]{:S(2)}) copy-start(f32[1024,32]{0,1:T(8,128)S(1)} %get-tuple-element.288) | copy-start | bytes 393220
  19.6 46.6 %copy-start.20 = (f32[1024,32]{0,1:T(8,128)}, f32[1024,32]{0,1:T(8,128)S(1)}, u32[]{:S(2)}) copy-start(f32[1024,32]{0,1:T(8,128)S(1)} %get-tuple-element.289) | copy-start | bytes 393220
  19.6 45.9 %copy-start.54 = (f32[64]{0:T(128)S(1)}, f32[64]{0:T(128)}, u32[]{:S(2)}) copy-start(f32[64]{0:T(128)} %param.24) | copy-start | bytes 772
  63.9 2.0 copy-start.7
  64.0 1.9 copy-start.40
  73.9 2.4 copy-start.26
  86.8 2.4 copy-start.26
  93.0 1.9 copy-start.11
  93.0 4.8 copy-start.39
  93.0 2.7 copy-start.28
  95.7 45.1 %copy-start.1 = (f32[256,1024]{1,0:T(8,128)S(1)}, f32[256,1024]{1,0:T(8,128)}, u32[]{:S(2)}) copy-start(f32[256,1024]{1,0:T(8,128)} %param.18) | copy-start | bytes 3145732
  97.8 44.3 %copy-start.42 = (f32[1024]{0:T(1024)S(1)}, f32[1024]{0:T(1024)}, u32[]{:S(2)}) copy-start(f32[1024]{0:T(1024)} %param.22) | copy-start | bytes 12292
  97.8 91.8 %all-gather.9.cloned.1.call-start = ((), (), s32[]{:S(2)}) async-start(), calls=%async_computation.6 | async-start | bytes 2621440 | tf_op jit(solution)/shard_map/all_gather | solution.py:139
  142.1 156.6 %copy-start.45 = (f32[256]{0:T(256)}, f32[256]{0:T(256)S(1)}, u32[]{:S(2)}) copy-start(f32[256]{0:T(256)S(1)} %fusion.72) | copy-start | bytes 3076
  144.1 92.4 %all-gather.11.cloned.1.call-start = ((), (), s32[]{:S(2)}) async-start(), calls=%async_computation.8 | async-start | bytes 2621440 | tf_op jit(solution)/shard_map/all_gather | solution.py:95
  144.7 151.6 %reduce-scatter.9.cloned.1.call-start = ((), (), s32[]{:S(2)}) async-start(), calls=%async_computation.9 | async-start | bytes 2621440 | tf_op jit(solution)/shard_map/reduce_scatter | solution.py:154
  189.5 7.5 %copy-start.58 = (bf16[1024,1152]{1,0:T(8,128)(2,1)S(1)}, bf16[1024,1152]{1,0:T(8,128)(2,1)}, u32[]{:S(2)}) copy-start(bf16[1024,1152]{1,0:T(8,128)(2,1)} %param.29) | copy-start | bytes 7077892
  189.6 7.5 %copy-start.63 = (bf16[1024,1024]{1,0:T(8,128)(2,1)S(1)}, bf16[1024,1024]{1,0:T(8,128)(2,1)}, u32[]{:S(2)}) copy-start(bf16[1024,1024]{1,0:T(8,128)(2,1)} %all-gather.9.cloned.1.call-done) | copy-start | bytes 6291460
  236.5 9.3 %copy-start.59 = (bf16[1024,1152]{1,0:T(8,128)(2,1)S(1)}, bf16[1024,1152]{1,0:T(8,128)(2,1)}, u32[]{:S(2)}) copy-start(bf16[1024,1152]{1,0:T(8,128)(2,1)} %param.29) | copy-start | bytes 7077892
  245.9 2.9 copy-start.66
  245.9 2.9 copy-start.68
  245.9 3.4 copy-start.60
  253.4 91.9 %all-gather.13.cloned.1.call-start = ((), (), s32[]{:S(2)}) async-start(), calls=%async_computation.10 | async-start | bytes 2621440 | tf_op jit(solution)/shard_map/all_gather | solution.py:170
  296.3 2.4 copy-start.10
  296.3 2.4 copy-start.14
  296.3 2.4 copy-start.15
  299.9 123.8 %all-reduce.8.cloned.1.call-start = ((), (), s32[]{:S(2)}) async-start(), calls=%async_computation.12 | async-start | bytes 4718592 | tf_op jit(solution)/shard_map/psum | solution.py:160
  307.3 220.0 %all-reduce.10.cloned.1.call-start = ((), (), s32[]{:S(2)}) async-start(), calls=%async_computation.13 | async-start | bytes 12582912 | tf_op jit(solution)/shard_map/psum | solution.py:240
  307.3 7.0 %copy-start.64 = (bf16[1024,1024]{1,0:T(8,128)(2,1)S(1)}, bf16[1024,1024]{1,0:T(8,128)(2,1)}, u32[]{:S(2)}) copy-start(bf16[1024,1024]{1,0:T(8,128)(2,1)} %all-gather.9.cloned.1.call-done) | copy-start | bytes 6291460
  307.3 6.9 %copy-start.67 = (bf16[1024,1152]{1,0:T(8,128)(2,1)S(1)}, bf16[1024,1152]{1,0:T(8,128)(2,1)}, u32[]{:S(2)}) copy-start(bf16[1024,1152]{1,0:T(8,128)(2,1)} %copy-done.66) | copy-start | bytes 7077892
  348.6 65.5 %copy-start.19 = (f32[1024,32]{0,1:T(8,128)S(1)}, f32[1024,32]{0,1:T(8,128)}, u32[]{:S(2)}) copy-start(f32[1024,32]{0,1:T(8,128)} %copy-done.18) | copy-start | bytes 393220
  353.3 2.5 copy-start.17
  355.9 3.3 copy-start.12
  362.7 2.4 copy-start.2
  362.7 2.4 copy-start.9
  383.8 2.5 copy-start.17
  386.3 4.4 copy-start.12
  394.2 2.4 copy-start.2
  394.2 2.4 copy-start.9
  411.0 5.7 copy-start.31
  414.1 2.6 copy-start.8
  414.1 2.7 slice-start.1
  414.1 2.7 copy-start.57
  417.5 1.9 copy-start.62
  418.8 2.2 copy-start.32
  419.0 2.0 copy-start.33
  419.5 2.0 copy-start.61
  423.7 149.9 %reduce-scatter.11.cloned.1.call-start = ((), (), s32[]{:S(2)}) async-start(), calls=%async_computation.11 | async-start | bytes 2621440 | tf_op jit(solution)/shard_map/reduce_scatter | solution.py:223
  428.0 225.9 %reduce-scatter.7.cloned.1.call-start = ((), (), s32[]{:S(2)}) async-start(), calls=%async_computation.7 | async-start | bytes 2621440 | tf_op jit(solution)/shard_map/reduce_scatter | solution.py:144
  527.3 4.4 copy-start.22
  531.7 2.6 copy-start.21
  534.3 2.5 copy-start.16
  534.3 39.3 %copy-start.44 = (f32[1024]{0:T(1024)S(1)}, f32[1024]{0:T(1024)}, u32[]{:S(2)}) copy-start(f32[1024]{0:T(1024)} %param.21) | copy-start | bytes 12292
  534.3 39.3 %copy-start.49 = (f32[256]{0:T(256)S(1)}, f32[256]{0:T(256)}, u32[]{:S(2)}) copy-start(f32[256]{0:T(256)} %copy-done.48) | copy-start | bytes 3076
  536.8 38.2 %copy-start.47 = (f32[1024]{0:T(1024)S(1)}, f32[1024]{0:T(1024)}, u32[]{:S(2)}) copy-start(f32[1024]{0:T(1024)} %get-tuple-element.211) | copy-start | bytes 12292
  536.8 116.0 %copy-start.51 = (f32[256]{0:T(256)S(1)}, f32[256]{0:T(256)}, u32[]{:S(2)}) copy-start(f32[256]{0:T(256)} %copy-done.50) | copy-start | bytes 3076
  536.8 117.2 %copy-start.43 = (f32[1024]{0:T(1024)S(1)}, f32[1024]{0:T(1024)}, u32[]{:S(2)}) copy-start(f32[1024]{0:T(1024)} %param.22) | copy-start | bytes 12292
  536.8 117.2 %copy-start.46 = (f32[256]{0:T(256)S(1)}, f32[256]{0:T(256)}, u32[]{:S(2)}) copy-start(f32[256]{0:T(256)} %copy-done.45) | copy-start | bytes 3076
  536.8 117.2 %copy-start.53 = (f32[256]{0:T(256)S(1)}, f32[256]{0:T(256)}, u32[]{:S(2)}) copy-start(f32[256]{0:T(256)} %copy-done.52) | copy-start | bytes 3076
  (25 other events, 29.7 us)
Sparse Core Ops, SparseCore 0:
  12.3 48.4 all-gather.6
  97.9 42.8 reduce-scatter.4
  144.2 45.2 all-gather.8
  191.6 44.8 all-gather.10
  253.5 42.7 reduce-scatter.8
  300.0 45.2 all-gather.12
  348.6 61.6 all-reduce.7
  423.9 103.3 all-reduce.9
  529.6 43.9 reduce-scatter.10
  575.8 45.6 reduce-scatter.6

commit v2 on v1

--- a/solution.py
+++ b/solution.py
@@ -1,3 +1,5 @@
+import functools
+
 import jax
 import jax.numpy as jnp
 from jax import lax
@@ -59,7 +61,35 @@
     )
 
 
+def gather_rows(block, shift_count):
+    blocks = [block]
+    for shift in range(1, shift_count):
+        pairs = [(i, (i + shift) % shift_count) for i in range(shift_count)]
+        blocks.append(lax.ppermute(block, "mp", pairs))
+    return jnp.concatenate(blocks, 0)
+
+
+def scatter_rows(block_of, shift_count):
+    order = sorted(range(1, shift_count), key=lambda shift: abs(2 * shift - shift_count))
+    total = 0.0
+    for shift in order:
+        pairs = [(i, (i - shift) % shift_count) for i in range(shift_count)]
+        sent = lax.ppermute(block_of(shift).astype(jnp.bfloat16), "mp", pairs)
+        total = total + sent.astype(jnp.float32)
+    return total + block_of(0)
+
+
+def butterfly(field, axis, size):
+    step = 1
+    while step < size:
+        field = field + lax.ppermute(field, axis, [(i, i ^ step) for i in range(size)])
+        step *= 2
+    return field
+
+
 def body(
+    mp_size,
+    dp_size,
     inputs,
     doc_ids,
     cotangent,
@@ -75,10 +105,16 @@
     up_weight,
     down_weight,
 ):
-    doc_full = doc_ids[0]
-    full_len = doc_full.shape[0]
-    where_full = positions(doc_full)
-    key_ids = jnp.arange(full_len, dtype=jnp.int32)
+    own_rows = inputs.shape[0]
+    full_len = doc_ids.shape[1]
+    turn = (lax.axis_index("mp") - jnp.arange(mp_size, dtype=jnp.int32)) % mp_size
+
+    def in_turn(field):
+        return field.reshape(mp_size, own_rows)[turn].reshape(full_len)
+
+    where_full = in_turn(positions(doc_ids[0]))
+    doc_full = in_turn(doc_ids[0])
+    key_ids = in_turn(jnp.arange(full_len, dtype=jnp.int32))
     query_cols = q_weight.shape[1]
     key_cols = k_weight.shape[1]
     query_heads = query_cols // HEAD
@@ -89,10 +125,10 @@
     block_count = full_len // block_rows
     block_starts = jnp.arange(block_count, dtype=jnp.int32) * block_rows
     normed_one, norm1_back = jax.vjp(normed, inputs, norm1_gain)
-    hidden = lax.all_gather(normed_one.astype(jnp.bfloat16), "mp", axis=0, tiled=True)
+    hidden = gather_rows(normed_one.astype(jnp.bfloat16), mp_size)
     joined = jnp.concatenate([q_weight, k_weight, v_weight], 1)
     hidden, cotangent_low = lax.optimization_barrier((hidden, cotangent.astype(jnp.bfloat16)))
-    grad_full = lax.all_gather(cotangent_low, "mp", axis=0, tiled=True)
+    grad_full = gather_rows(cotangent_low, mp_size)
     projected = dot_plain(hidden, joined)
     query_raw = projected[:, :query_cols].reshape(full_len, query_heads, HEAD)
     key_raw = projected[:, query_cols : query_cols + key_cols].reshape(full_len, kv_heads, HEAD)
@@ -114,7 +150,7 @@
             jnp.einsum("qkgd,skd->kgqs", query_block, keys_all, preferred_element_type=jnp.float32)
             * score_scale
         )
-        row_ids = begin_row + jnp.arange(block_rows, dtype=jnp.int32)
+        row_ids = lax.dynamic_slice_in_dim(key_ids, begin_row, block_rows, 0)
         doc_block = lax.dynamic_slice_in_dim(doc_full, begin_row, block_rows, 0)
         allowed = (doc_block[:, None] == doc_full[None, :]) & (key_ids[None, :] <= row_ids[:, None])
         return (jnp.where(allowed, raw_scores, -1e30), query_block)
@@ -131,19 +167,21 @@
         return (block_out, (row_max + jnp.log(row_total))[..., 0])
 
     block_out, log_totals = lax.map(forward_block, block_starts)
+    block_out, log_totals, grad_full = lax.optimization_barrier((block_out, log_totals, grad_full))
     attended = block_out.reshape(full_len, query_cols).astype(jnp.bfloat16)
-    mid_rows = inputs + lax.psum_scatter(
-        dot_plain(attended, o_weight).astype(jnp.bfloat16), "mp", scatter_dimension=0, tiled=True
-    ).astype(jnp.float32)
+
+    def rows_of(field, shift):
+        return field[shift * own_rows : (shift + 1) * own_rows]
+
+    mid_rows = inputs + scatter_rows(
+        lambda shift: dot_plain(rows_of(attended, shift), o_weight), mp_size
+    )
     normed_two, norm2_back = jax.vjp(normed, mid_rows, norm2_gain)
-    hidden_mid = lax.all_gather(normed_two.astype(jnp.bfloat16), "mp", axis=0, tiled=True)
+    hidden_mid = gather_rows(normed_two.astype(jnp.bfloat16), mp_size)
     gate_pre = dot_plain(hidden_mid, gate_weight)
     up_pre = dot_plain(hidden_mid, up_weight)
     activated, gated_back = jax.vjp(gated, gate_pre, up_pre)
     act_low = activated.astype(jnp.bfloat16)
-    result = mid_rows + lax.psum_scatter(
-        dot_plain(act_low, down_weight).astype(jnp.bfloat16), "mp", scatter_dimension=0, tiled=True
-    ).astype(jnp.float32)
     grad_act = dot_right_t(grad_full, down_weight)
     down_wgrad = dot_left_t(act_low, grad_full)
     grad_gate, grad_up = gated_back(grad_act)
@@ -151,12 +189,11 @@
     grad_up = grad_up.astype(jnp.bfloat16)
     gate_wgrad = dot_left_t(hidden_mid, grad_gate)
     up_wgrad = dot_left_t(hidden_mid, grad_up)
-    grad_normed_mid = lax.psum_scatter(
-        (dot_right_t(grad_gate, gate_weight) + dot_right_t(grad_up, up_weight)).astype(jnp.bfloat16),
-        "mp",
-        scatter_dimension=0,
-        tiled=True,
-    ).astype(jnp.float32)
+    grad_normed_mid = scatter_rows(
+        lambda shift: dot_right_t(rows_of(grad_gate, shift), gate_weight)
+        + dot_right_t(rows_of(grad_up, shift), up_weight),
+        mp_size,
+    )
     down_total, gate_total, up_total = lax.psum(
         (
             down_wgrad.astype(jnp.bfloat16),
@@ -167,7 +204,11 @@
     )
     grad_mid_norm, gain2_grad = norm2_back(grad_normed_mid)
     grad_mid = cotangent + grad_mid_norm
-    grad_mid_full = lax.all_gather(grad_mid.astype(jnp.bfloat16), "mp", axis=0, tiled=True)
+    grad_mid_full = gather_rows(grad_mid.astype(jnp.bfloat16), mp_size)
+    grad_mid_full, act_late = lax.optimization_barrier((grad_mid_full, act_low))
+    result = mid_rows + scatter_rows(
+        lambda shift: dot_plain(rows_of(act_late, shift), down_weight), mp_size
+    )
     grad_att = (
         dot_right_t(grad_mid_full, o_weight)
         .astype(jnp.bfloat16)
@@ -208,6 +249,9 @@
     zero_kv = jnp.zeros((full_len, kv_heads, HEAD), jnp.float32)
     (grad_keys, grad_values), grad_queries = lax.scan(
         backward_block, (zero_kv, zero_kv), (block_starts, log_totals)
+    )
+    grad_queries, grad_keys, grad_values, result = lax.optimization_barrier(
+        (grad_queries, grad_keys, grad_values, result)
     )
     grad_qraw, qgain_grad = query_back(grad_queries.reshape(full_len, query_heads, HEAD))
     grad_kraw, kgain_grad = key_back(grad_keys)
@@ -220,22 +264,31 @@
         1,
     ).astype(jnp.bfloat16)
     joined_wgrad = dot_left_t(hidden, grad_joined)
-    grad_normed_in = lax.psum_scatter(
-        dot_right_t(grad_joined, joined).astype(jnp.bfloat16), "mp", scatter_dimension=0, tiled=True
-    ).astype(jnp.float32)
+    grad_normed_in = scatter_rows(
+        lambda shift: dot_right_t(rows_of(grad_joined, shift), joined), mp_size
+    )
+    joined_low, out_low, down_total, gate_total, up_total = lax.optimization_barrier(
+        (
+            joined_wgrad.astype(jnp.bfloat16),
+            out_wgrad.astype(jnp.bfloat16),
+            down_total,
+            gate_total,
+            up_total,
+        )
+    )
+    grad_normed_in, _, _, _ = lax.optimization_barrier(
+        (grad_normed_in, joined_low, out_low, down_total)
+    )
     grad_in_norm, gain1_grad = norm1_back(grad_normed_in)
     inputs_grad = grad_mid + grad_in_norm
     gains = jnp.concatenate([gain1_grad, gain2_grad, qgain_grad, kgain_grad])
-    gains = jnp.sum(lax.all_gather(gains, ("dp", "mp"), axis=0), 0)
+    gains = butterfly(butterfly(gains, "dp", dp_size), "mp", mp_size)
     width = gain1_grad.shape[0]
     gain_totals = (
         gains[:width],
         gains[width : 2 * width],
         gains[2 * width : 2 * width + HEAD],
         gains[2 * width + HEAD :],
-    )
-    joined_low, out_low, down_total = lax.optimization_barrier(
-        (joined_wgrad.astype(jnp.bfloat16), out_wgrad.astype(jnp.bfloat16), down_total)
     )
     joined_wgrad, out_wgrad = lax.psum((joined_low, out_low), "dp")
     joined_wgrad = joined_wgrad.astype(jnp.float32)
@@ -295,4 +348,5 @@
         P(None, "mp"),
         P("mp", None),
     )
-    return jax.shard_map(body, mesh=mesh, in_specs=in_specs, out_specs=out_specs, check_vma=False)
+    local = functools.partial(body, mesh.shape["mp"], mesh.shape["dp"])
+    return jax.shard_map(local, mesh=mesh, in_specs=in_specs, out_specs=out_specs, check_vma=False)

time: 675 us -> 552 us (0.82)
  waiting for transfers between devices: 358 us -> 216 us
  starting transfers between devices: 0.58 us -> 120 us
  blocking collectives: 76.6 us -> 0 us
  local copies, waits for them, and re-layouts: 49.9 us -> 29.8 us
  other arithmetic: 51.2 us -> 43.2 us
    ppermute x0 -> x29, waiting for transfers between devices: none -> 178 us  [the longest x12 86.5 us: gather_rows(): blocks.append(lax.ppermute(block, 'mp', pairs))]
    all_gather x4 -> x0, waiting for transfers between devices: 148 us -> none  [the longest x1 44.6 us: body(): lax.all_gather(normed_two.astype(jnp.bfloat16), 'mp', axis=0, tiled=True)]
    reduce_scatter x4 -> x0, waiting for transfers between devices: 122 us -> none  [the longest x1 43 us: body(): lax.psum_scatter(dot_plain(attended, o_weight).astype(jnp.bfloat16), 'mp'...]
    ppermute x0 -> x29, starting transfers between devices: none -> 120 us  [the longest x12 56.6 us: gather_rows(): blocks.append(lax.ppermute(block, 'mp', pairs))]
    all_gather x1 -> x0, blocking collectives: 76.6 us -> none  [body(): gains = jnp.sum(lax.all_gather(gains, ('dp', 'mp'), axis=0), 0)]
    psum x1, waiting for transfers between devices: 88.7 us -> 38.4 us  [body(): joined_wgrad, out_wgrad = lax.psum((joined_low, out_low), 'dp')]
    dynamic_update_slice x4 -> x0, local copies, waits for them, and re-layouts: 23.5 us -> none  [body(): block_out, log_totals = lax.map(forward_block, block_starts)]
    dot_general x5 -> x11, matrix products: 23.3 us -> 31.7 us  [dot_plain(): return jnp.dot(left, right, preferred_element_type=jnp.float32)]
  transfers between devices with their start and end apart: 10 -> 31, of which waited for: 8 -> 17; matrix products, arithmetic and copies ran while one was open for 20% -> 24% of each run, Pallas kernels for 0% -> 0%
where the time goes in v2:
time: 552 us; the launch traced here: 543 us
  waiting for transfers between devices  216 us (39%)
  starting transfers between devices  120 us (22%)
  matrix products  109 us (20%)
  other arithmetic  43.2 us (8%)
  local copies, waits for them, and re-layouts  29.8 us (5%)
  between operations  16.1 us (3%)
  loops' own time  8.2 us (1%)
    ppermute x12, waiting for transfers between devices, gather_rows(): blocks.append(lax.ppermute(block, 'mp', pairs))  86.5 us
    ppermute x12, waiting for transfers between devices, scatter_rows(): sent = lax.ppermute(block_of(shift).astype(jnp.bfloat16), 'mp', pairs)  84.1 us
    ppermute x12, starting transfers between devices, gather_rows(): blocks.append(lax.ppermute(block, 'mp', pairs))  56.6 us
    ppermute x12, starting transfers between devices, scatter_rows(): sent = lax.ppermute(block_of(shift).astype(jnp.bfloat16), 'mp', pairs)  46.8 us
    psum x1, waiting for transfers between devices, body(): joined_wgrad, out_wgrad = lax.psum((joined_low, out_low), 'dp')  38.4 us
    dot_general x11, matrix products, dot_plain(): return jnp.dot(left, right, preferred_element_type=jnp.float32)  31.7 us
    dot_general x14, matrix products, dot_right_t(): lax.dot_general(left, right, (((1,), (1,)), ((), ())), preferred_element_...  18.2 us
    ppermute x5, starting transfers between devices, butterfly(): lax.ppermute(field, axis, [(i, i ^ step) for i in range(size)])  16.8 us
  transfers between devices with their start and end apart: 31, of which 17 were waited for; matrix products, arithmetic and copies ran while one was open for 24% of the time, Pallas kernels for 0%

profile of v2, /device:TPU:0, one launch (start us, length us, event | category | flops | bytes accessed | tf_op | source)
XLA Modules:
  0.0 542.7 jit_solution(11104499190373342219)
XLA Ops:
  10.2 3.1 collective-permute-start
  13.3 2.6 collective-permute-start.1
  29.9 20.0 %collective-permute-done.1 = bf16[256,1024]{1,0:T(8,128)(2,1)} collective-permute-done((bf16[256,1024]{1,0:T(8,128)(2,1)S(1)}, bf16[256,1024]{1,0:T(8,128)(2,1)}, u32[]{:S(2)}, u32[]{:S(2)}) %collective-permute-start.1) | collective-permute-done | bytes 524320 | tf_op jit(solution)/shard_map/ppermute | solution.py:68
  53.1 11.8 %collective-permute-start.3 = (bf16[256,1024]{1,0:T(8,128)(2,1)}, bf16[256,1024]{1,0:T(8,128)(2,1)}, u32[]{:S(2)}, u32[]{:S(2)}) collective-permute-start(bf16[256,1024]{1,0:T(8,128)(2,1)} %convert_element_type.158), channel_id=1, source_target_pairs={{0,1},{1,2},{2,3},{3,0},{4,5},{5,6},{6,7},{7,4},{8,9},{9,10},{10,1... | collective-permute-start | bytes 1572872 | tf_op jit(solution)/shard_map/ppermute | solution.py:68
  68.8 22.1 %while.29 = (s32[]{:T(128)}, bf16[2,512,2,2,64]{1,4,3,2,0:T(8,128)(2,1)}, f32[2,2,2,512]{3,2,1,0:T(2,128)S(1)}, s32[2]{0:T(128)S(1)}, s32[1024]{0:T(1024)S(1)}, ...) while((s32[]{:T(128)}, ...), condition=%wide.region_8.9_spmd.clone, body=%wide.region_5.8_spmd.sunk.clone | while | flops 563607552 | bytes 28676780 | solution.py:169
  73.9 2.4 fusion.181
  76.3 3.5 fusion.182
  85.0 2.4 fusion.181
  87.4 3.5 fusion.182
  90.9 8.9 %collective-permute-done.4 = bf16[256,1024]{1,0:T(8,128)(2,1)} collective-permute-done((bf16[256,1024]{1,0:T(8,128)(2,1)}, bf16[256,1024]{1,0:T(8,128)(2,1)}, u32[]{:S(2)}, u32[]{:S(2)}) %collective-permute-start.4) | collective-permute-done | bytes 524320 | tf_op jit(solution)/shard_map/ppermute | solution.py:68
  99.8 3.0 pad_maximum_fusion.1
  107.9 10.7 %collective-permute-start.6 = (bf16[256,1024]{1,0:T(8,128)(2,1)}, bf16[256,1024]{1,0:T(8,128)(2,1)}, u32[]{:S(2)}, u32[]{:S(2)}) collective-permute-start(bf16[256,1024]{1,0:T(8,128)(2,1)} %convolution_convert_fusion.12), channel_id=1, source_target_pairs={{0,2},{1,3},{2,0},{3,1},{4,6},{5,7},{6,4},{7,5},{8,10},{9,11},{10,... | collective-permute-start | bytes 1572872 | tf_op jit(solution)/shard_map/ppermute | solution.py:77
  118.6 3.4 collective-permute-start.7
  122.0 20.8 %collective-permute-done.6 = bf16[256,1024]{1,0:T(8,128)(2,1)} collective-permute-done((bf16[256,1024]{1,0:T(8,128)(2,1)}, bf16[256,1024]{1,0:T(8,128)(2,1)}, u32[]{:S(2)}, u32[]{:S(2)}) %collective-permute-start.6) | collective-permute-done | bytes 524320 | tf_op jit(solution)/shard_map/ppermute | solution.py:77
  142.9 13.9 %collective-permute-done.8 = bf16[256,1024]{1,0:T(8,128)(2,1)} collective-permute-done((bf16[256,1024]{1,0:T(8,128)(2,1)}, bf16[256,1024]{1,0:T(8,128)(2,1)}, u32[]{:S(2)}, u32[]{:S(2)}) %collective-permute-start.8) | collective-permute-done | bytes 524320 | tf_op jit(solution)/shard_map/ppermute | solution.py:77
  158.9 10.7 %collective-permute-start.10 = (bf16[256,1024]{1,0:T(8,128)(2,1)S(1)}, bf16[256,1024]{1,0:T(8,128)(2,1)S(1)}, u32[]{:S(2)}, u32[]{:S(2)}) collective-permute-start(bf16[256,1024]{1,0:T(8,128)(2,1)S(1)} %multiply_convert_fusion.2), channel_id=1, source_target_pairs={{0,2},{1,3},{2,0},{3,1},{4,6},{5,7},{6,4},{7,5},{8,10},{9,11},{10,... | collective-permute-start | bytes 1572872 | tf_op jit(solution)/shard_map/ppermute | solution.py:68
  172.1 2.9 fusion.108
  175.0 19.2 %collective-permute-done.10 = bf16[256,1024]{1,0:T(8,128)(2,1)S(1)} collective-permute-done((bf16[256,1024]{1,0:T(8,128)(2,1)S(1)}, bf16[256,1024]{1,0:T(8,128)(2,1)S(1)}, u32[]{:S(2)}, u32[]{:S(2)}) %collective-permute-start.10) | collective-permute-done | bytes 524320 | tf_op jit(solution)/shard_map/ppermute | solution.py:68
  194.2 11.2 %collective-permute-done.11 = bf16[256,1024]{1,0:T(8,128)(2,1)S(1)} collective-permute-done((bf16[256,1024]{1,0:T(8,128)(2,1)S(1)}, bf16[256,1024]{1,0:T(8,128)(2,1)S(1)}, u32[]{:S(2)}, u32[]{:S(2)}) %collective-permute-start.11) | collective-permute-done | bytes 524320 | tf_op jit(solution)/shard_map/ppermute | solution.py:68
  205.4 6.1 %fusion.100 = f32[1024,1152]{1,0:T(8,128)} fusion(bf16[1024,1152]{1,0:T(8,128)(2,1)S(1)} %copy-done.4, bf16[256,1024]{1,0:T(8,128)(2,1)S(1)} %collective-permute-done.11, bf16[256,1024]{1,0:T(8,128)(2,1)S(1)} %collective-permute-done.10, bf16[256,1024]{1,0:T(8,128)(2,1)S(1)} %collective-permute-done.9, bf16[256,1024]{1,0:T(8,128)(2,1)S(1)} %multiply_convert_fusion.2), kind=kOutput, calls=%fused_computation.195 | convolution fusion | flops 2424307712 | bytes 9175040 | tf_op jit(solution)/shard_map/dot_general | solution.py:49
  211.5 8.1 %multiply_convert_fusion = (bf16[1024,1152]{1,0:T(8,128)(2,1)S(1)}, bf16[1024,1152]{1,0:T(8,128)(2,1)S(1)}, bf16[1024,1152]{1,0:T(8,128)(2,1)S(1)}) fusion(f32[1024,1152]{1,0:T(8,128)} %fusion.100, f32[1024,1152]{1,0:T(8,128)S(1)} %fusion.108, bf16[1024,1152]{1,0:T(8,128)(2,1)S(1)} %copy-done, bf16[256,1024]{1,0:T(8,128)(2,1)S(1)} %collective-permute-done.11, ...), kind=kOutput, calls=%fused_computation.61 | convolution fusion | flops 2443182080 | bytes 20971520 | tf_op jit(solution)/shard_map/dot_general | solution.py:49
  224.0 9.7 %collective-permute-start.12 = (bf16[256,1024]{1,0:T(8,128)(2,1)S(1)}, bf16[256,1024]{1,0:T(8,128)(2,1)S(1)}, u32[]{:S(2)}, u32[]{:S(2)}) collective-permute-start(bf16[256,1024]{1,0:T(8,128)(2,1)S(1)} %fusion.50), channel_id=1, source_target_pairs={{0,2},{1,3},{2,0},{3,1},{4,6},{5,7},{6,4},{7,5},{8,10},{9,11},{10,... | collective-permute-start | bytes 1572872 | tf_op jit(solution)/shard_map/ppermute | solution.py:77
  234.6 3.4 collective-permute-start.13
  239.2 4.3 convolution_convert_fusion
  243.4 4.2 convolution_convert_fusion.1
  247.7 10.0 %collective-permute-done.12 = bf16[256,1024]{1,0:T(8,128)(2,1)S(1)} collective-permute-done((bf16[256,1024]{1,0:T(8,128)(2,1)S(1)}, bf16[256,1024]{1,0:T(8,128)(2,1)S(1)}, u32[]{:S(2)}, u32[]{:S(2)}) %collective-permute-start.12) | collective-permute-done | bytes 524320 | tf_op jit(solution)/shard_map/ppermute | solution.py:77
  257.7 13.7 %collective-permute-done.14 = bf16[256,1024]{1,0:T(8,128)(2,1)S(1)} collective-permute-done((bf16[256,1024]{1,0:T(8,128)(2,1)S(1)}, bf16[256,1024]{1,0:T(8,128)(2,1)S(1)}, u32[]{:S(2)}, u32[]{:S(2)}) %collective-permute-start.14) | collective-permute-done | bytes 524320 | tf_op jit(solution)/shard_map/ppermute | solution.py:77
  274.0 19.8 %collective-permute-start.15 = (bf16[256,1024]{1,0:T(8,128)(2,1)}, bf16[256,1024]{1,0:T(8,128)(2,1)}, u32[]{:S(2)}, u32[]{:S(2)}) collective-permute-start(bf16[256,1024]{1,0:T(8,128)(2,1)} %get-tuple-element.292), channel_id=1, source_target_pairs={{0,1},{1,2},{2,3},{3,0},{4,5},{5,6},{6,7},{7,4},{8,9},{9,10},{10,1... | collective-permute-start | bytes 1572872 | tf_op jit(solution)/shard_map/ppermute | solution.py:68
  293.8 2.4 collective-permute-start.17
  296.2 3.9 convolution_convert_fusion.2
  300.1 6.4 %collective-permute-done.15 = bf16[256,1024]{1,0:T(8,128)(2,1)} collective-permute-done((bf16[256,1024]{1,0:T(8,128)(2,1)}, bf16[256,1024]{1,0:T(8,128)(2,1)}, u32[]{:S(2)}, u32[]{:S(2)}) %collective-permute-start.15) | collective-permute-done | bytes 524320 | tf_op jit(solution)/shard_map/ppermute | solution.py:68
  306.5 12.4 %collective-permute-done.16 = bf16[256,1024]{1,0:T(8,128)(2,1)} collective-permute-done((bf16[256,1024]{1,0:T(8,128)(2,1)}, bf16[256,1024]{1,0:T(8,128)(2,1)}, u32[]{:S(2)}, u32[]{:S(2)}) %collective-permute-start.16) | collective-permute-done | bytes 524320 | tf_op jit(solution)/shard_map/ppermute | solution.py:68
  318.9 8.4 %collective-permute-done.17 = bf16[256,1024]{1,0:T(8,128)(2,1)} collective-permute-done((bf16[256,1024]{1,0:T(8,128)(2,1)}, bf16[256,1024]{1,0:T(8,128)(2,1)}, u32[]{:S(2)}, u32[]{:S(2)}) %collective-permute-start.17) | collective-permute-done | bytes 524320 | tf_op jit(solution)/shard_map/ppermute | solution.py:68
  329.0 3.3 convolution_convert_fusion.9
  335.8 3.5 collective-permute-start.18
  339.3 10.9 %collective-permute-start.19 = (bf16[256,1024]{1,0:T(8,128)(2,1)}, bf16[256,1024]{1,0:T(8,128)(2,1)}, u32[]{:S(2)}, u32[]{:S(2)}) collective-permute-start(bf16[256,1024]{1,0:T(8,128)(2,1)} %convolution_convert_fusion.8), channel_id=1, source_target_pairs={{0,3},{1,0},{2,1},{3,2},{4,7},{5,4},{6,5},{7,6},{8,11},{9,8},{10,9... | collective-permute-start | bytes 1572872 | tf_op jit(solution)/shard_map/ppermute | solution.py:77
  352.3 48.5 %while.30 = (s32[]{:T(128)}, f32[1024,2,64]{0,2,1:T(8,128)S(1)}, f32[1024,2,64]{0,2,1:T(8,128)}, f32[2,512,2,2,64]{1,4,3,2,0:T(8,128)}, s32[2]{0:T(128)S(1)}, /*...) while((s32[]{:T(128)}, f32[1024,2,64]{0,2,1:T(8,128)S(1)}, ...), condition=%wide.region_13.14_spmd.clone.clone, body=%wide.region_11.13_spmd.clone.sunk.clone | while | flops 1375991808 | bytes 124089160 | solution.py:250
  357.0 3.5 fusion.192
  360.5 2.4 fusion.193
  364.9 2.2 fusion.196
  367.1 3.2 fusion.194
  370.3 5.6 %fusion.195 = f32[1024,2,64]{0,2,1:T(8,128)} fusion(f32[2,512,2,1024]{3,1,2,0:T(8,128)} %copy-done.2, f32[2,2,512]{2,1,0:T(2,128)S(1)} %dynamic-slice_bitcast_fusion.3, pred[512,1024]{1,0:T(8,128)(4,1)S(1)} %compare_and_fusion.7, f32[1024,2,64]{0,2,1:T(8,128)} %get-tuple-element.591, pred[]{:T(512)S(6)} %compare.15, ...), kind=kOutput, calls=%fused_computation.40.clone.1.clone | convolution fusion | flops 277086208 | bytes 10231813 | tf_op jit(solution)/shard_map/while/body/eval_jaxpr/kgqs,qkgd->skd/dot_general | solution.py:241
  380.6 3.5 fusion.192
  384.7 2.4 fusion.193
  389.1 2.2 fusion.196
  391.3 3.3 fusion.194
  394.6 5.9 %fusion.195 = f32[1024,2,64]{0,2,1:T(8,128)} fusion(f32[2,512,2,1024]{3,1,2,0:T(8,128)} %copy-done.2, f32[2,2,512]{2,1,0:T(2,128)S(1)} %dynamic-slice_bitcast_fusion.3, pred[512,1024]{1,0:T(8,128)(4,1)S(1)} %compare_and_fusion.7, f32[1024,2,64]{0,2,1:T(8,128)} %get-tuple-element.591, pred[]{:T(512)S(6)} %compare.15, ...), kind=kOutput, calls=%fused_computation.40.clone.1.clone | convolution fusion | flops 277086208 | bytes 10231813 | tf_op jit(solution)/shard_map/while/body/eval_jaxpr/kgqs,qkgd->skd/dot_general | solution.py:241
  400.8 4.2 add_add_fusion.4
  405.1 3.0 copy.28
  408.1 3.2 reshape.329
  419.0 3.1 collective-permute-start.22
  425.0 2.3 convolution_convert_fusion.3
  427.3 25.6 %collective-permute-done.21 = bf16[256,1024]{1,0:T(8,128)(2,1)S(1)} collective-permute-done((bf16[256,1024]{1,0:T(8,128)(2,1)}, bf16[256,1024]{1,0:T(8,128)(2,1)S(1)}, u32[]{:S(2)}, u32[]{:S(2)}) %collective-permute-start.21) | collective-permute-done | bytes 524320 | tf_op jit(solution)/shard_map/ppermute | solution.py:77
  452.9 2.6 add_add_fusion.3
  459.9 2.1 collective-permute-done.25
  463.6 2.1 collective-permute-done.26
  465.8 10.5 %collective-permute-start.27 = (f32[2176]{0:T(1024)S(1)}, f32[2176]{0:T(1024)S(1)}, u32[]{:S(2)}, u32[]{:S(2)}) collective-permute-start(f32[2176]{0:T(1024)S(1)} %add.250), channel_id=1, source_target_pairs={{0,1},{1,0},{2,3},{3,2},{4,5},{5,4},{6,7},{7,6},{8,9},{9,8},{10,11... | collective-permute-start | bytes 26120 | tf_op jit(solution)/shard_map/ppermute | solution.py:85
  477.9 3.2 collective-permute-start.28
  481.1 2.5 fusion.55
  483.6 2.7 convert_element_type.202
  486.3 2.5 convert_element_type.200
  489.0 2.5 convert_element_type.201
  492.7 38.4 %all-reduce.9.cloned.1.call-done = (bf16[1024,512]{1,0:T(8,128)(2,1)}, bf16[256,1024]{1,0:T(8,128)(2,1)}) async-done(((bf16[1024,512]{1,0:T(8,128)(2,1)}, bf16[256,1024]{1,0:T(8,128)(2,1)}), (bf16[1024,512]{1,0:T(8,128)(2,1)}, bf16[256,1024]{1,0:T(8,128)(2,1)})) %all-reduce.9.cloned.1.call-update) | async-done | bytes 1572880 | tf_op jit(solution)/shard_map/psum | solution.py:293
  531.1 2.2 fusion.104
  (309 shorter events, 86.9 us)
Async XLA Ops:
  7.2 204.3 %copy-start = (bf16[1024,1152]{1,0:T(8,128)(2,1)S(1)}, bf16[1024,1152]{1,0:T(8,128)(2,1)}, u32[]{:S(2)}) copy-start(bf16[1024,1152]{1,0:T(8,128)(2,1)} %param.30) | copy-start | bytes 7077892
  7.2 14.5 %copy-start.46 = (bf16[1024,128]{1,0:T(8,128)(2,1)S(1)}, bf16[1024,128]{1,0:T(8,128)(2,1)}, u32[]{:S(2)}) copy-start(bf16[1024,128]{1,0:T(8,128)(2,1)} %param.26) | copy-start | bytes 786436
  7.2 448.3 %all-reduce.11.cloned.1.call-start = ((), (), s32[]{:S(2)}) async-start(), calls=%async_computation.1 | async-start | bytes 14155776 | tf_op jit(solution)/shard_map/psum | solution.py:197
  10.2 19.7 %collective-permute-start = (bf16[256,1024]{1,0:T(8,128)(2,1)S(1)}, bf16[256,1024]{1,0:T(8,128)(2,1)}, u32[]{:S(2)}, u32[]{:S(2)}) collective-permute-start(bf16[256,1024]{1,0:T(8,128)(2,1)S(1)} %multiply_convert_fusion.3), channel_id=1, source_target_pairs={{0,1},{1,2},{2,3},{3,0},{4,5},{5,6},{6,7},{7,4},{8,9},{9,10},{10,1... | collective-permute-start | bytes 1572872 | tf_op jit(solution)/shard_map/ppermute | solution.py:68
  13.3 36.7 %collective-permute-start.1 = (bf16[256,1024]{1,0:T(8,128)(2,1)S(1)}, bf16[256,1024]{1,0:T(8,128)(2,1)}, u32[]{:S(2)}, u32[]{:S(2)}) collective-permute-start(bf16[256,1024]{1,0:T(8,128)(2,1)S(1)} %multiply_convert_fusion.3), channel_id=1, source_target_pairs={{0,2},{1,3},{2,0},{3,1},{4,6},{5,7},{6,4},{7,5},{8,10},{9,11},{10,... | collective-permute-start | bytes 1572872 | tf_op jit(solution)/shard_map/ppermute | solution.py:68
  15.9 34.1 %collective-permute-start.2 = (bf16[256,1024]{1,0:T(8,128)(2,1)S(1)}, bf16[256,1024]{1,0:T(8,128)(2,1)}, u32[]{:S(2)}, u32[]{:S(2)}) collective-permute-start(bf16[256,1024]{1,0:T(8,128)(2,1)S(1)} %multiply_convert_fusion.3), channel_id=1, source_target_pairs={{0,3},{1,0},{2,1},{3,2},{4,7},{5,4},{6,5},{7,6},{8,11},{9,8},{10,9... | collective-permute-start | bytes 1572872 | tf_op jit(solution)/shard_map/ppermute | solution.py:68
  29.3 22.1 %copy-start.11 = (bf16[1024,512]{1,0:T(8,128)(2,1)S(1)}, bf16[1024,512]{1,0:T(8,128)(2,1)}, u32[]{:S(2)}) copy-start(bf16[1024,512]{1,0:T(8,128)(2,1)} %constant_dynamic-update-slice_fusion) | copy-start | bytes 3145732
  29.9 38.7 %copy-start.26 = (f32[1024,32]{0,1:T(8,128)}, f32[1024,32]{0,1:T(8,128)S(1)}, u32[]{:S(2)}) copy-start(f32[1024,32]{0,1:T(8,128)S(1)} %get-tuple-element.315) | copy-start | bytes 393220
  29.9 38.7 %copy-start.28 = (f32[1024,32]{0,1:T(8,128)}, f32[1024,32]{0,1:T(8,128)S(1)}, u32[]{:S(2)}) copy-start(f32[1024,32]{0,1:T(8,128)S(1)} %get-tuple-element.316) | copy-start | bytes 393220
  51.5 16.4 %copy-start.62 = (f32[64]{0:T(128)S(1)}, f32[64]{0:T(128)}, u32[]{:S(2)}) copy-start(f32[64]{0:T(128)} %param.24) | copy-start | bytes 772
  52.8 15.4 %copy-start.5 = (f32[1024,512]{0,1:T(8,128)}, f32[1024,512]{0,1:T(8,128)S(1)}, u32[]{:S(2)}) copy-start(f32[1024,512]{0,1:T(8,128)S(1)} %fusion.107) | copy-start | bytes 6291460
  52.8 15.2 %copy-start.64 = (f32[64]{0:T(128)S(1)}, f32[64]{0:T(128)}, u32[]{:S(2)}) copy-start(f32[64]{0:T(128)} %param.23) | copy-start | bytes 772
  52.9 15.4 %copy-start.53 = (f32[1024,2]{0,1:T(2,128)}, f32[1024,2]{0,1:T(2,128)S(1)}, u32[]{:S(2)}) copy-start(f32[1024,2]{0,1:T(2,128)S(1)} %multiply_reduce_fusion.11) | copy-start | bytes 24580
  53.0 14.3 %copy-start.47 = (f32[1024,4]{0,1:T(4,128)}, f32[1024,4]{0,1:T(4,128)S(1)}, u32[]{:S(2)}) copy-start(f32[1024,4]{0,1:T(4,128)S(1)} %multiply_reduce_fusion.7) | copy-start | bytes 49156
  53.1 37.8 %collective-permute-start.3 = (bf16[256,1024]{1,0:T(8,128)(2,1)}, bf16[256,1024]{1,0:T(8,128)(2,1)}, u32[]{:S(2)}, u32[]{:S(2)}) collective-permute-start(bf16[256,1024]{1,0:T(8,128)(2,1)} %convert_element_type.158), channel_id=1, source_target_pairs={{0,1},{1,2},{2,3},{3,0},{4,5},{5,6},{6,7},{7,4},{8,9},{9,10},{10,1... | collective-permute-start | bytes 1572872 | tf_op jit(solution)/shard_map/ppermute | solution.py:68
  64.8 35.0 %collective-permute-start.4 = (bf16[256,1024]{1,0:T(8,128)(2,1)}, bf16[256,1024]{1,0:T(8,128)(2,1)}, u32[]{:S(2)}, u32[]{:S(2)}) collective-permute-start(bf16[256,1024]{1,0:T(8,128)(2,1)} %convert_element_type.158), channel_id=1, source_target_pairs={{0,2},{1,3},{2,0},{3,1},{4,6},{5,7},{6,4},{7,5},{8,10},{9,11},{10,... | collective-permute-start | bytes 1572872 | tf_op jit(solution)/shard_map/ppermute | solution.py:68
  66.4 33.4 %collective-permute-start.5 = (bf16[256,1024]{1,0:T(8,128)(2,1)}, bf16[256,1024]{1,0:T(8,128)(2,1)}, u32[]{:S(2)}, u32[]{:S(2)}) collective-permute-start(bf16[256,1024]{1,0:T(8,128)(2,1)} %convert_element_type.158), channel_id=1, source_target_pairs={{0,3},{1,0},{2,1},{3,2},{4,7},{5,4},{6,5},{7,6},{8,11},{9,8},{10,9... | collective-permute-start | bytes 1572872 | tf_op jit(solution)/shard_map/ppermute | solution.py:68
  90.9 13.5 %copy-start.14 = (bf16[1024,2,2,64]{0,3,2,1:T(8,128)(2,1)}, bf16[1024,2,2,64]{0,3,2,1:T(8,128)(2,1)S(1)}, u32[]{:S(2)}) copy-start(bf16[1024,2,2,64]{0,3,2,1:T(8,128)(2,1)S(1)} %get-tuple-element.628) | copy-start | bytes 1572868
  90.9 13.6 %copy-start.17 = (bf16[256,1024]{1,0:T(8,128)(2,1)S(1)}, bf16[256,1024]{1,0:T(8,128)(2,1)}, u32[]{:S(2)}) copy-start(bf16[256,1024]{1,0:T(8,128)(2,1)} %param.28) | copy-start | bytes 1572868
  107.9 35.0 %collective-permute-start.6 = (bf16[256,1024]{1,0:T(8,128)(2,1)}, bf16[256,1024]{1,0:T(8,128)(2,1)}, u32[]{:S(2)}, u32[]{:S(2)}) collective-permute-start(bf16[256,1024]{1,0:T(8,128)(2,1)} %convolution_convert_fusion.12), channel_id=1, source_target_pairs={{0,2},{1,3},{2,0},{3,1},{4,6},{5,7},{6,4},{7,5},{8,10},{9,11},{10,... | collective-permute-start | bytes 1572872 | tf_op jit(solution)/shard_map/ppermute | solution.py:77
  118.6 24.3 %collective-permute-start.7 = (bf16[256,1024]{1,0:T(8,128)(2,1)}, bf16[256,1024]{1,0:T(8,128)(2,1)}, u32[]{:S(2)}, u32[]{:S(2)}) collective-permute-start(bf16[256,1024]{1,0:T(8,128)(2,1)} %convolution_convert_fusion.11), channel_id=1, source_target_pairs={{0,3},{1,0},{2,1},{3,2},{4,7},{5,4},{6,5},{7,6},{8,11},{9,8},{10,9... | collective-permute-start | bytes 1572872 | tf_op jit(solution)/shard_map/ppermute | solution.py:77
  122.0 34.8 %collective-permute-start.8 = (bf16[256,1024]{1,0:T(8,128)(2,1)}, bf16[256,1024]{1,0:T(8,128)(2,1)}, u32[]{:S(2)}, u32[]{:S(2)}) collective-permute-start(bf16[256,1024]{1,0:T(8,128)(2,1)} %convolution_convert_fusion.10), channel_id=1, source_target_pairs={{0,1},{1,2},{2,3},{3,0},{4,5},{5,6},{6,7},{7,4},{8,9},{9,10},{10,1... | collective-permute-start | bytes 1572872 | tf_op jit(solution)/shard_map/ppermute | solution.py:77
  122.0 34.8 %copy-start.9 = (f32[256,1024]{1,0:T(8,128)S(1)}, f32[256,1024]{1,0:T(8,128)}, u32[]{:S(2)}) copy-start(f32[256,1024]{1,0:T(8,128)} %param.18) | copy-start | bytes 3145732
  122.0 34.8 %copy-start.18 = (bf16[256,1024]{1,0:T(8,128)(2,1)S(1)}, bf16[256,1024]{1,0:T(8,128)(2,1)}, u32[]{:S(2)}) copy-start(bf16[256,1024]{1,0:T(8,128)(2,1)} %param.28) | copy-start | bytes 1572868
  122.0 36.7 %copy-start.55 = (f32[1024]{0:T(1024)S(1)}, f32[1024]{0:T(1024)}, u32[]{:S(2)}) copy-start(f32[1024]{0:T(1024)} %param.22) | copy-start | bytes 12292
  122.0 50.1 %copy-start.30 = (bf16[1152,1024]{1,0:T(8,128)(2,1)S(1)}, bf16[1152,1024]{1,0:T(8,128)(2,1)}, u32[]{:S(2)}) copy-start(bf16[1152,1024]{1,0:T(8,128)(2,1)} %param.31) | copy-start | bytes 7077892
  122.0 50.1 %copy-start.42 = (bf16[1024,1024]{1,0:T(8,128)(2,1)S(1)}, bf16[1024,1024]{1,0:T(8,128)(2,1)}, u32[]{:S(2)}) copy-start(bf16[1024,1024]{1,0:T(8,128)(2,1)} %pad_maximum_fusion.1) | copy-start | bytes 6291460
  158.7 113.9 %copy-start.7 = (f32[256,1024]{1,0:T(8,128)}, f32[256,1024]{1,0:T(8,128)S(1)}, u32[]{:S(2)}) copy-start(f32[256,1024]{1,0:T(8,128)S(1)} %get-tuple-element.318) | copy-start | bytes 3145732
  158.9 46.5 %copy-start.4 = (bf16[1024,1152]{1,0:T(8,128)(2,1)S(1)}, bf16[1024,1152]{1,0:T(8,128)(2,1)}, u32[]{:S(2)}) copy-start(bf16[1024,1152]{1,0:T(8,128)(2,1)} %param.29) | copy-start | bytes 7077892
  158.9 35.3 %collective-permute-start.10 = (bf16[256,1024]{1,0:T(8,128)(2,1)S(1)}, bf16[256,1024]{1,0:T(8,128)(2,1)S(1)}, u32[]{:S(2)}, u32[]{:S(2)}) collective-permute-start(bf16[256,1024]{1,0:T(8,128)(2,1)S(1)} %multiply_convert_fusion.2), channel_id=1, source_target_pairs={{0,2},{1,3},{2,0},{3,1},{4,6},{5,7},{6,4},{7,5},{8,10},{9,11},{10,... | collective-permute-start | bytes 1572872 | tf_op jit(solution)/shard_map/ppermute | solution.py:68
  169.6 35.8 %collective-permute-start.11 = (bf16[256,1024]{1,0:T(8,128)(2,1)S(1)}, bf16[256,1024]{1,0:T(8,128)(2,1)S(1)}, u32[]{:S(2)}, u32[]{:S(2)}) collective-permute-start(bf16[256,1024]{1,0:T(8,128)(2,1)S(1)} %multiply_convert_fusion.2), channel_id=1, source_target_pairs={{0,3},{1,0},{2,1},{3,2},{4,7},{5,4},{6,5},{7,6},{8,11},{9,8},{10,9... | collective-permute-start | bytes 1572872 | tf_op jit(solution)/shard_map/ppermute | solution.py:68
  170.0 35.3 %collective-permute-start.9 = (bf16[256,1024]{1,0:T(8,128)(2,1)S(1)}, bf16[256,1024]{1,0:T(8,128)(2,1)S(1)}, u32[]{:S(2)}, u32[]{:S(2)}) collective-permute-start(bf16[256,1024]{1,0:T(8,128)(2,1)S(1)} %multiply_convert_fusion.2), channel_id=1, source_target_pairs={{0,1},{1,2},{2,3},{3,0},{4,5},{5,6},{6,7},{7,4},{8,9},{9,10},{10,1... | collective-permute-start | bytes 1572872 | tf_op jit(solution)/shard_map/ppermute | solution.py:68
  219.6 76.5 %copy-start.49 = (bf16[1024,1152]{1,0:T(8,128)(2,1)}, bf16[1024,1152]{1,0:T(8,128)(2,1)S(1)}, u32[]{:S(2)}) copy-start(bf16[1024,1152]{1,0:T(8,128)(2,1)S(1)} %get-tuple-element.173) | copy-start | bytes 7077892
  224.0 33.7 %collective-permute-start.12 = (bf16[256,1024]{1,0:T(8,128)(2,1)S(1)}, bf16[256,1024]{1,0:T(8,128)(2,1)S(1)}, u32[]{:S(2)}, u32[]{:S(2)}) collective-permute-start(bf16[256,1024]{1,0:T(8,128)(2,1)S(1)} %fusion.50), channel_id=1, source_target_pairs={{0,2},{1,3},{2,0},{3,1},{4,6},{5,7},{6,4},{7,5},{8,10},{9,11},{10,... | collective-permute-start | bytes 1572872 | tf_op jit(solution)/shard_map/ppermute | solution.py:77
  234.6 23.1 %collective-permute-start.13 = (bf16[256,1024]{1,0:T(8,128)(2,1)S(1)}, bf16[256,1024]{1,0:T(8,128)(2,1)S(1)}, u32[]{:S(2)}, u32[]{:S(2)}) collective-permute-start(bf16[256,1024]{1,0:T(8,128)(2,1)S(1)} %fusion.51), channel_id=1, source_target_pairs={{0,3},{1,0},{2,1},{3,2},{4,7},{5,4},{6,5},{7,6},{8,11},{9,8},{10,9... | collective-permute-start | bytes 1572872 | tf_op jit(solution)/shard_map/ppermute | solution.py:77
  238.9 32.4 %collective-permute-start.14 = (bf16[256,1024]{1,0:T(8,128)(2,1)S(1)}, bf16[256,1024]{1,0:T(8,128)(2,1)S(1)}, u32[]{:S(2)}, u32[]{:S(2)}) collective-permute-start(bf16[256,1024]{1,0:T(8,128)(2,1)S(1)} %fusion.52), channel_id=1, source_target_pairs={{0,1},{1,2},{2,3},{3,0},{4,5},{5,6},{6,7},{7,4},{8,9},{9,10},{10,1... | collective-permute-start | bytes 1572872 | tf_op jit(solution)/shard_map/ppermute | solution.py:77
  247.7 24.9 %copy-start.20 = (f32[256,1024]{1,0:T(8,128)S(1)}, f32[256,1024]{1,0:T(8,128)}, u32[]{:S(2)}) copy-start(f32[256,1024]{1,0:T(8,128)} %param.20) | copy-start | bytes 3145732
  274.0 32.5 %collective-permute-start.15 = (bf16[256,1024]{1,0:T(8,128)(2,1)}, bf16[256,1024]{1,0:T(8,128)(2,1)}, u32[]{:S(2)}, u32[]{:S(2)}) collective-permute-start(bf16[256,1024]{1,0:T(8,128)(2,1)} %get-tuple-element.292), channel_id=1, source_target_pairs={{0,1},{1,2},{2,3},{3,0},{4,5},{5,6},{6,7},{7,4},{8,9},{9,10},{10,1... | collective-permute-start | bytes 1572872 | tf_op jit(solution)/shard_map/ppermute | solution.py:68
  293.8 25.1 %collective-permute-start.16 = (bf16[256,1024]{1,0:T(8,128)(2,1)}, bf16[256,1024]{1,0:T(8,128)(2,1)}, u32[]{:S(2)}, u32[]{:S(2)}) collective-permute-start(bf16[256,1024]{1,0:T(8,128)(2,1)} %get-tuple-element.292), channel_id=1, source_target_pairs={{0,2},{1,3},{2,0},{3,1},{4,6},{5,7},{6,4},{7,5},{8,10},{9,11},{10,... | collective-permute-start | bytes 1572872 | tf_op jit(solution)/shard_map/ppermute | solution.py:68
  293.8 33.5 %collective-permute-start.17 = (bf16[256,1024]{1,0:T(8,128)(2,1)}, bf16[256,1024]{1,0:T(8,128)(2,1)}, u32[]{:S(2)}, u32[]{:S(2)}) collective-permute-start(bf16[256,1024]{1,0:T(8,128)(2,1)} %get-tuple-element.292), channel_id=1, source_target_pairs={{0,3},{1,0},{2,1},{3,2},{4,7},{5,4},{6,5},{7,6},{8,11},{9,8},{10,9... | collective-permute-start | bytes 1572872 | tf_op jit(solution)/shard_map/ppermute | solution.py:68
  300.1 28.9 %copy-start.31 = (bf16[1152,1024]{1,0:T(8,128)(2,1)S(1)}, bf16[1152,1024]{1,0:T(8,128)(2,1)}, u32[]{:S(2)}) copy-start(bf16[1152,1024]{1,0:T(8,128)(2,1)} %param.31) | copy-start | bytes 7077892
  300.1 231.0 %all-reduce.9.cloned.1.call-start = ((), (), s32[]{:S(2)}) async-start(), calls=%async_computation | async-start | bytes 3145728 | tf_op jit(solution)/shard_map/psum | solution.py:293
  329.0 21.8 %copy-start.40 = (bf16[1024,1024]{1,0:T(8,128)(2,1)}, bf16[1024,1024]{1,0:T(8,128)(2,1)S(1)}, u32[]{:S(2)}) copy-start(bf16[1024,1024]{1,0:T(8,128)(2,1)S(1)} %pad_maximum_fusion.3) | copy-start | bytes 6291460
  334.1 16.7 %copy-start.19 = (bf16[256,1024]{1,0:T(8,128)(2,1)S(1)}, bf16[256,1024]{1,0:T(8,128)(2,1)}, u32[]{:S(2)}) copy-start(bf16[256,1024]{1,0:T(8,128)(2,1)} %param.28) | copy-start | bytes 1572868
  335.8 16.6 %copy-start.15 = (bf16[1024,2,2,64]{0,3,2,1:T(8,128)(2,1)S(1)}, bf16[1024,2,2,64]{0,3,2,1:T(8,128)(2,1)}, u32[]{:S(2)}) copy-start(bf16[1024,2,2,64]{0,3,2,1:T(8,128)(2,1)} %copy-done.14) | copy-start | bytes 1572868
  335.8 65.0 %collective-permute-start.18 = (bf16[256,1024]{1,0:T(8,128)(2,1)}, bf16[256,1024]{1,0:T(8,128)(2,1)}, u32[]{:S(2)}, u32[]{:S(2)}) collective-permute-start(bf16[256,1024]{1,0:T(8,128)(2,1)} %convolution_convert_fusion.9), channel_id=1, source_target_pairs={{0,2},{1,3},{2,0},{3,1},{4,6},{5,7},{6,4},{7,5},{8,10},{9,11},{10,... | collective-permute-start | bytes 1572872 | tf_op jit(solution)/shard_map/ppermute | solution.py:77
  339.3 61.5 %collective-permute-start.19 = (bf16[256,1024]{1,0:T(8,128)(2,1)}, bf16[256,1024]{1,0:T(8,128)(2,1)}, u32[]{:S(2)}, u32[]{:S(2)}) collective-permute-start(bf16[256,1024]{1,0:T(8,128)(2,1)} %convolution_convert_fusion.8), channel_id=1, source_target_pairs={{0,3},{1,0},{2,1},{3,2},{4,7},{5,4},{6,5},{7,6},{8,11},{9,8},{10,9... | collective-permute-start | bytes 1572872 | tf_op jit(solution)/shard_map/ppermute | solution.py:77
  350.2 50.7 %collective-permute-start.20 = (bf16[256,1024]{1,0:T(8,128)(2,1)}, bf16[256,1024]{1,0:T(8,128)(2,1)}, u32[]{:S(2)}, u32[]{:S(2)}) collective-permute-start(bf16[256,1024]{1,0:T(8,128)(2,1)} %convolution_convert_fusion.7), channel_id=1, source_target_pairs={{0,1},{1,2},{2,3},{3,0},{4,5},{5,6},{6,7},{7,4},{8,9},{9,10},{10,1... | collective-permute-start | bytes 1572872 | tf_op jit(solution)/shard_map/ppermute | solution.py:77
  352.3 48.5 %copy-start.8 = (f32[256,1024]{1,0:T(8,128)S(1)}, f32[256,1024]{1,0:T(8,128)}, u32[]{:S(2)}) copy-start(f32[256,1024]{1,0:T(8,128)} %copy-done.7) | copy-start | bytes 3145732
  416.5 36.4 %collective-permute-start.21 = (bf16[256,1024]{1,0:T(8,128)(2,1)}, bf16[256,1024]{1,0:T(8,128)(2,1)S(1)}, u32[]{:S(2)}, u32[]{:S(2)}) collective-permute-start(bf16[256,1024]{1,0:T(8,128)(2,1)} %convolution_convert_fusion.6), channel_id=1, source_target_pairs={{0,2},{1,3},{2,0},{3,1},{4,6},{5,7},{6,4},{7,5},{8,10},{9,11},{10,... | collective-permute-start | bytes 1572872 | tf_op jit(solution)/shard_map/ppermute | solution.py:77
  419.0 33.9 %collective-permute-start.22 = (bf16[256,1024]{1,0:T(8,128)(2,1)}, bf16[256,1024]{1,0:T(8,128)(2,1)S(1)}, u32[]{:S(2)}, u32[]{:S(2)}) collective-permute-start(bf16[256,1024]{1,0:T(8,128)(2,1)} %convolution_convert_fusion.5), channel_id=1, source_target_pairs={{0,3},{1,0},{2,1},{3,2},{4,7},{5,4},{6,5},{7,6},{8,11},{9,8},{10,9... | collective-permute-start | bytes 1572872 | tf_op jit(solution)/shard_map/ppermute | solution.py:77
  423.4 29.5 %collective-permute-start.23 = (bf16[256,1024]{1,0:T(8,128)(2,1)}, bf16[256,1024]{1,0:T(8,128)(2,1)}, u32[]{:S(2)}, u32[]{:S(2)}) collective-permute-start(bf16[256,1024]{1,0:T(8,128)(2,1)} %convolution_convert_fusion.4), channel_id=1, source_target_pairs={{0,1},{1,2},{2,3},{3,0},{4,5},{5,6},{6,7},{7,4},{8,9},{9,10},{10,1... | collective-permute-start | bytes 1572872 | tf_op jit(solution)/shard_map/ppermute | solution.py:77
  424.9 28.0 %copy-start.13 = (bf16[1024,512]{1,0:T(8,128)(2,1)S(1)}, bf16[1024,512]{1,0:T(8,128)(2,1)}, u32[]{:S(2)}) copy-start(bf16[1024,512]{1,0:T(8,128)(2,1)} %constant_dynamic-update-slice_fusion) | copy-start | bytes 3145732
  427.3 28.2 %copy-start.10 = (f32[256,1024]{1,0:T(8,128)S(1)}, f32[256,1024]{1,0:T(8,128)}, u32[]{:S(2)}) copy-start(f32[256,1024]{1,0:T(8,128)} %param.18) | copy-start | bytes 3145732
  427.3 28.2 %copy-start.56 = (f32[1024]{0:T(1024)S(1)}, f32[1024]{0:T(1024)}, u32[]{:S(2)}) copy-start(f32[1024]{0:T(1024)} %param.21) | copy-start | bytes 12292
  427.3 28.3 %copy-start.59 = (f32[256]{0:T(256)S(1)}, f32[256]{0:T(256)}, u32[]{:S(2)}) copy-start(f32[256]{0:T(256)} %copy-done.58) | copy-start | bytes 3076
  455.5 20.7 %copy-start.61 = (f32[256]{0:T(256)S(1)}, f32[256]{0:T(256)}, u32[]{:S(2)}) copy-start(f32[256]{0:T(256)} %copy-done.60) | copy-start | bytes 3076
  455.5 25.6 %copy-start.16 = (f32[256,1024]{1,0:T(8,128)S(1)}, f32[256,1024]{1,0:T(8,128)}, u32[]{:S(2)}) copy-start(f32[256,1024]{1,0:T(8,128)} %add_add_fusion.3) | copy-start | bytes 3145732
  457.2 1.2 collective-permute-start.24
  458.4 3.7 collective-permute-start.25
  462.1 3.7 collective-permute-start.26
  463.6 20.0 %copy-start.35 = (bf16[1152,1024]{1,0:T(8,128)(2,1)S(1)}, bf16[1152,1024]{1,0:T(8,128)(2,1)}, u32[]{:S(2)}) copy-start(bf16[1152,1024]{1,0:T(8,128)(2,1)} %get-tuple-element.180) | copy-start | bytes 7077892
  465.8 12.1 %collective-permute-start.27 = (f32[2176]{0:T(1024)S(1)}, f32[2176]{0:T(1024)S(1)}, u32[]{:S(2)}, u32[]{:S(2)}) collective-permute-start(f32[2176]{0:T(1024)S(1)} %add.250), channel_id=1, source_target_pairs={{0,1},{1,0},{2,3},{3,2},{4,5},{5,4},{6,7},{7,6},{8,9},{9,8},{10,11... | collective-permute-start | bytes 26120 | tf_op jit(solution)/shard_map/ppermute | solution.py:85
  477.9 13.6 %collective-permute-start.28 = (f32[2176]{0:T(1024)S(1)}, f32[2176]{0:T(1024)S(1)}, u32[]{:S(2)}, u32[]{:S(2)}) collective-permute-start(f32[2176]{0:T(1024)S(1)} %add.251), channel_id=1, source_target_pairs={{0,2},{1,3},{2,0},{3,1},{4,6},{5,7},{6,4},{7,5},{8,10},{9,11},{10,... | collective-permute-start | bytes 26120 | tf_op jit(solution)/shard_map/ppermute | solution.py:85
  (39 other events, 148.6 us)
Sparse Core Ops, SparseCore 0:
  300.2 112.9 all-reduce.10
  463.7 67.3 all-reduce.8

commit v3 on v2

--- a/solution.py
+++ b/solution.py
@@ -264,9 +264,6 @@
         1,
     ).astype(jnp.bfloat16)
     joined_wgrad = dot_left_t(hidden, grad_joined)
-    grad_normed_in = scatter_rows(
-        lambda shift: dot_right_t(rows_of(grad_joined, shift), joined), mp_size
-    )
     joined_low, out_low, down_total, gate_total, up_total = lax.optimization_barrier(
         (
             joined_wgrad.astype(jnp.bfloat16),
@@ -276,13 +273,20 @@
             up_total,
         )
     )
-    grad_normed_in, _, _, _ = lax.optimization_barrier(
-        (grad_normed_in, joined_low, out_low, down_total)
+    joined_late, _, _, _ = lax.optimization_barrier((grad_joined, joined_low, out_low, down_total))
+    grad_normed_in = scatter_rows(
+        lambda shift: dot_right_t(
+            rows_of(joined_late if shift in (0, mp_size - 1) else grad_joined, shift), joined
+        ),
+        mp_size,
     )
     grad_in_norm, gain1_grad = norm1_back(grad_normed_in)
     inputs_grad = grad_mid + grad_in_norm
     gains = jnp.concatenate([gain1_grad, gain2_grad, qgain_grad, kgain_grad])
-    gains = butterfly(butterfly(gains, "dp", dp_size), "mp", mp_size)
+    joined_wgrad, out_wgrad = lax.psum((joined_low, out_low), "dp")
+    gains = butterfly(gains, "dp", dp_size)
+    gains, joined_wgrad, out_wgrad = lax.optimization_barrier((gains, joined_wgrad, out_wgrad))
+    gains = butterfly(gains, "mp", mp_size)
     width = gain1_grad.shape[0]
     gain_totals = (
         gains[:width],
@@ -290,7 +294,6 @@
         gains[2 * width : 2 * width + HEAD],
         gains[2 * width + HEAD :],
     )
-    joined_wgrad, out_wgrad = lax.psum((joined_low, out_low), "dp")
     joined_wgrad = joined_wgrad.astype(jnp.float32)
     out_wgrad = out_wgrad.astype(jnp.float32)
     gate_wgrad = gate_total.astype(jnp.float32)

time: 552 us -> 517 us (0.937)
  waiting for transfers between devices: 216 us -> 190 us
  starting transfers between devices: 120 us -> 110 us
    psum x1, waiting for transfers between devices: 38.4 us -> 15.7 us  [body(): joined_wgrad, out_wgrad = lax.psum((joined_low, out_low), 'dp')]
    ppermute x5, starting transfers between devices: 16.8 us -> 6.86 us  [butterfly(): lax.ppermute(field, axis, [(i, i ^ step) for i in range(size)])]
  transfers between devices with their start and end apart: 31 -> 31, of which waited for: 17 -> 15; matrix products, arithmetic and copies ran while one was open for 24% -> 27% of each run, Pallas kernels for 0% -> 0%
where the time goes in v3:
time: 517 us; the launch traced here: 508 us
  waiting for transfers between devices  190 us (37%)
  starting transfers between devices  110 us (21%)
  matrix products  110 us (21%)
  other arithmetic  43.2 us (8%)
  local copies, waits for them, and re-layouts  29.4 us (6%)
  between operations  16.1 us (3%)
  loops' own time  8.17 us (2%)
    ppermute x12, waiting for transfers between devices, gather_rows(): blocks.append(lax.ppermute(block, 'mp', pairs))  86.5 us
    ppermute x12, waiting for transfers between devices, scatter_rows(): sent = lax.ppermute(block_of(shift).astype(jnp.bfloat16), 'mp', pairs)  84.5 us
    ppermute x12, starting transfers between devices, gather_rows(): blocks.append(lax.ppermute(block, 'mp', pairs))  56.6 us
    ppermute x12, starting transfers between devices, scatter_rows(): sent = lax.ppermute(block_of(shift).astype(jnp.bfloat16), 'mp', pairs)  47 us
    dot_general x11, matrix products, dot_plain(): return jnp.dot(left, right, preferred_element_type=jnp.float32)  30.9 us
    dot_general x14, matrix products, dot_right_t(): lax.dot_general(left, right, (((1,), (1,)), ((), ())), preferred_element_...  18.6 us
    dot_general x5, matrix products, dot_left_t(): lax.dot_general(left, right, (((0,), (0,)), ((), ())), preferred_element_...  18 us
    psum x1, waiting for transfers between devices, body(): joined_wgrad, out_wgrad = lax.psum((joined_low, out_low), 'dp')  15.7 us
  transfers between devices with their start and end apart: 31, of which 15 were waited for; matrix products, arithmetic and copies ran while one was open for 27% of the time, Pallas kernels for 0%

profile of v3, /device:TPU:0, one launch (start us, length us, event | category | flops | bytes accessed | tf_op | source)
XLA Modules:
  0.0 507.9 jit_solution(16678438097114678264)
XLA Ops:
  10.2 3.1 collective-permute-start
  13.3 2.6 collective-permute-start.1
  22.4 2.1 convert_element_type.158
  29.9 20.0 %collective-permute-done.1 = bf16[256,1024]{1,0:T(8,128)(2,1)} collective-permute-done((bf16[256,1024]{1,0:T(8,128)(2,1)S(1)}, bf16[256,1024]{1,0:T(8,128)(2,1)}, u32[]{:S(2)}, u32[]{:S(2)}) %collective-permute-start.1) | collective-permute-done | bytes 524320 | tf_op jit(solution)/shard_map/ppermute | solution.py:68
  53.1 11.8 %collective-permute-start.3 = (bf16[256,1024]{1,0:T(8,128)(2,1)}, bf16[256,1024]{1,0:T(8,128)(2,1)}, u32[]{:S(2)}, u32[]{:S(2)}) collective-permute-start(bf16[256,1024]{1,0:T(8,128)(2,1)} %convert_element_type.158), channel_id=1, source_target_pairs={{0,1},{1,2},{2,3},{3,0},{4,5},{5,6},{6,7},{7,4},{8,9},{9,10},{10,1... | collective-permute-start | bytes 1572872 | tf_op jit(solution)/shard_map/ppermute | solution.py:68
  68.8 22.1 %while.29 = (s32[]{:T(128)}, bf16[2,512,2,2,64]{1,4,3,2,0:T(8,128)(2,1)}, f32[2,2,2,512]{3,2,1,0:T(2,128)S(1)}, s32[2]{0:T(128)S(1)}, s32[1024]{0:T(1024)S(1)}, ...) while((s32[]{:T(128)}, ...), condition=%wide.region_8.9_spmd.clone, body=%wide.region_5.8_spmd.sunk.clone | while | flops 563607552 | bytes 28676780 | solution.py:169
  73.9 2.4 fusion.181
  76.3 3.5 fusion.182
  85.0 2.4 fusion.181
  87.4 3.5 fusion.182
  90.9 8.9 %collective-permute-done.4 = bf16[256,1024]{1,0:T(8,128)(2,1)} collective-permute-done((bf16[256,1024]{1,0:T(8,128)(2,1)}, bf16[256,1024]{1,0:T(8,128)(2,1)}, u32[]{:S(2)}, u32[]{:S(2)}) %collective-permute-start.4) | collective-permute-done | bytes 524320 | tf_op jit(solution)/shard_map/ppermute | solution.py:68
  99.8 3.0 pad_maximum_fusion.1
  107.9 10.7 %collective-permute-start.6 = (bf16[256,1024]{1,0:T(8,128)(2,1)}, bf16[256,1024]{1,0:T(8,128)(2,1)}, u32[]{:S(2)}, u32[]{:S(2)}) collective-permute-start(bf16[256,1024]{1,0:T(8,128)(2,1)} %convolution_convert_fusion.12), channel_id=1, source_target_pairs={{0,2},{1,3},{2,0},{3,1},{4,6},{5,7},{6,4},{7,5},{8,10},{9,11},{10,... | collective-permute-start | bytes 1572872 | tf_op jit(solution)/shard_map/ppermute | solution.py:77
  118.6 3.4 collective-permute-start.7
  122.0 20.8 %collective-permute-done.6 = bf16[256,1024]{1,0:T(8,128)(2,1)} collective-permute-done((bf16[256,1024]{1,0:T(8,128)(2,1)}, bf16[256,1024]{1,0:T(8,128)(2,1)}, u32[]{:S(2)}, u32[]{:S(2)}) %collective-permute-start.6) | collective-permute-done | bytes 524320 | tf_op jit(solution)/shard_map/ppermute | solution.py:77
  142.9 13.9 %collective-permute-done.8 = bf16[256,1024]{1,0:T(8,128)(2,1)} collective-permute-done((bf16[256,1024]{1,0:T(8,128)(2,1)}, bf16[256,1024]{1,0:T(8,128)(2,1)}, u32[]{:S(2)}, u32[]{:S(2)}) %collective-permute-start.8) | collective-permute-done | bytes 524320 | tf_op jit(solution)/shard_map/ppermute | solution.py:77
  158.9 10.7 %collective-permute-start.10 = (bf16[256,1024]{1,0:T(8,128)(2,1)S(1)}, bf16[256,1024]{1,0:T(8,128)(2,1)S(1)}, u32[]{:S(2)}, u32[]{:S(2)}) collective-permute-start(bf16[256,1024]{1,0:T(8,128)(2,1)S(1)} %multiply_convert_fusion.2), channel_id=1, source_target_pairs={{0,2},{1,3},{2,0},{3,1},{4,6},{5,7},{6,4},{7,5},{8,10},{9,11},{10,... | collective-permute-start | bytes 1572872 | tf_op jit(solution)/shard_map/ppermute | solution.py:68
  172.1 2.9 fusion.108
  175.0 19.2 %collective-permute-done.10 = bf16[256,1024]{1,0:T(8,128)(2,1)S(1)} collective-permute-done((bf16[256,1024]{1,0:T(8,128)(2,1)S(1)}, bf16[256,1024]{1,0:T(8,128)(2,1)S(1)}, u32[]{:S(2)}, u32[]{:S(2)}) %collective-permute-start.10) | collective-permute-done | bytes 524320 | tf_op jit(solution)/shard_map/ppermute | solution.py:68
  194.2 11.2 %collective-permute-done.11 = bf16[256,1024]{1,0:T(8,128)(2,1)S(1)} collective-permute-done((bf16[256,1024]{1,0:T(8,128)(2,1)S(1)}, bf16[256,1024]{1,0:T(8,128)(2,1)S(1)}, u32[]{:S(2)}, u32[]{:S(2)}) %collective-permute-start.11) | collective-permute-done | bytes 524320 | tf_op jit(solution)/shard_map/ppermute | solution.py:68
  205.4 6.1 %fusion.100 = f32[1024,1152]{1,0:T(8,128)} fusion(bf16[1024,1152]{1,0:T(8,128)(2,1)S(1)} %copy-done.4, bf16[256,1024]{1,0:T(8,128)(2,1)S(1)} %collective-permute-done.11, bf16[256,1024]{1,0:T(8,128)(2,1)S(1)} %collective-permute-done.10, bf16[256,1024]{1,0:T(8,128)(2,1)S(1)} %collective-permute-done.9, bf16[256,1024]{1,0:T(8,128)(2,1)S(1)} %multiply_convert_fusion.2), kind=kOutput, calls=%fused_computation.195 | convolution fusion | flops 2424307712 | bytes 9175040 | tf_op jit(solution)/shard_map/dot_general | solution.py:49
  211.5 8.1 %multiply_convert_fusion = (bf16[1024,1152]{1,0:T(8,128)(2,1)S(1)}, bf16[1024,1152]{1,0:T(8,128)(2,1)S(1)}, bf16[1024,1152]{1,0:T(8,128)(2,1)S(1)}) fusion(f32[1024,1152]{1,0:T(8,128)} %fusion.100, f32[1024,1152]{1,0:T(8,128)S(1)} %fusion.108, bf16[1024,1152]{1,0:T(8,128)(2,1)S(1)} %copy-done, bf16[256,1024]{1,0:T(8,128)(2,1)S(1)} %collective-permute-done.11, ...), kind=kOutput, calls=%fused_computation.61 | convolution fusion | flops 2443182080 | bytes 20971520 | tf_op jit(solution)/shard_map/dot_general | solution.py:49
  224.0 9.7 %collective-permute-start.12 = (bf16[256,1024]{1,0:T(8,128)(2,1)S(1)}, bf16[256,1024]{1,0:T(8,128)(2,1)S(1)}, u32[]{:S(2)}, u32[]{:S(2)}) collective-permute-start(bf16[256,1024]{1,0:T(8,128)(2,1)S(1)} %fusion.50), channel_id=1, source_target_pairs={{0,2},{1,3},{2,0},{3,1},{4,6},{5,7},{6,4},{7,5},{8,10},{9,11},{10,... | collective-permute-start | bytes 1572872 | tf_op jit(solution)/shard_map/ppermute | solution.py:77
  234.6 3.4 collective-permute-start.13
  239.2 4.2 convolution_convert_fusion
  243.4 4.3 convolution_convert_fusion.1
  247.7 10.0 %collective-permute-done.12 = bf16[256,1024]{1,0:T(8,128)(2,1)S(1)} collective-permute-done((bf16[256,1024]{1,0:T(8,128)(2,1)S(1)}, bf16[256,1024]{1,0:T(8,128)(2,1)S(1)}, u32[]{:S(2)}, u32[]{:S(2)}) %collective-permute-start.12) | collective-permute-done | bytes 524320 | tf_op jit(solution)/shard_map/ppermute | solution.py:77
  257.7 13.7 %collective-permute-done.14 = bf16[256,1024]{1,0:T(8,128)(2,1)S(1)} collective-permute-done((bf16[256,1024]{1,0:T(8,128)(2,1)S(1)}, bf16[256,1024]{1,0:T(8,128)(2,1)S(1)}, u32[]{:S(2)}, u32[]{:S(2)}) %collective-permute-start.14) | collective-permute-done | bytes 524320 | tf_op jit(solution)/shard_map/ppermute | solution.py:77
  274.0 19.8 %collective-permute-start.15 = (bf16[256,1024]{1,0:T(8,128)(2,1)}, bf16[256,1024]{1,0:T(8,128)(2,1)}, u32[]{:S(2)}, u32[]{:S(2)}) collective-permute-start(bf16[256,1024]{1,0:T(8,128)(2,1)} %get-tuple-element.298), channel_id=1, source_target_pairs={{0,1},{1,2},{2,3},{3,0},{4,5},{5,6},{6,7},{7,4},{8,9},{9,10},{10,1... | collective-permute-start | bytes 1572872 | tf_op jit(solution)/shard_map/ppermute | solution.py:68
  293.8 2.4 collective-permute-start.17
  296.2 3.9 convolution_convert_fusion.2
  300.1 6.4 %collective-permute-done.15 = bf16[256,1024]{1,0:T(8,128)(2,1)} collective-permute-done((bf16[256,1024]{1,0:T(8,128)(2,1)}, bf16[256,1024]{1,0:T(8,128)(2,1)}, u32[]{:S(2)}, u32[]{:S(2)}) %collective-permute-start.15) | collective-permute-done | bytes 524320 | tf_op jit(solution)/shard_map/ppermute | solution.py:68
  306.5 12.4 %collective-permute-done.16 = bf16[256,1024]{1,0:T(8,128)(2,1)} collective-permute-done((bf16[256,1024]{1,0:T(8,128)(2,1)}, bf16[256,1024]{1,0:T(8,128)(2,1)}, u32[]{:S(2)}, u32[]{:S(2)}) %collective-permute-start.16) | collective-permute-done | bytes 524320 | tf_op jit(solution)/shard_map/ppermute | solution.py:68
  318.9 8.4 %collective-permute-done.17 = bf16[256,1024]{1,0:T(8,128)(2,1)} collective-permute-done((bf16[256,1024]{1,0:T(8,128)(2,1)}, bf16[256,1024]{1,0:T(8,128)(2,1)}, u32[]{:S(2)}, u32[]{:S(2)}) %collective-permute-start.17) | collective-permute-done | bytes 524320 | tf_op jit(solution)/shard_map/ppermute | solution.py:68
  329.0 3.3 convolution_convert_fusion.9
  335.7 3.5 collective-permute-start.18
  339.3 10.9 %collective-permute-start.19 = (bf16[256,1024]{1,0:T(8,128)(2,1)}, bf16[256,1024]{1,0:T(8,128)(2,1)}, u32[]{:S(2)}, u32[]{:S(2)}) collective-permute-start(bf16[256,1024]{1,0:T(8,128)(2,1)} %convolution_convert_fusion.8), channel_id=1, source_target_pairs={{0,3},{1,0},{2,1},{3,2},{4,7},{5,4},{6,5},{7,6},{8,11},{9,8},{10,9... | collective-permute-start | bytes 1572872 | tf_op jit(solution)/shard_map/ppermute | solution.py:77
  351.5 48.2 %while.30 = (s32[]{:T(128)}, f32[1024,2,64]{0,2,1:T(8,128)S(1)}, f32[1024,2,64]{0,2,1:T(8,128)}, f32[2,512,2,2,64]{1,4,3,2,0:T(8,128)}, s32[2]{0:T(128)S(1)}, /*...) while((s32[]{:T(128)}, f32[1024,2,64]{0,2,1:T(8,128)S(1)}, ...), condition=%wide.region_13.14_spmd.clone.clone, body=%wide.region_11.13_spmd.clone.sunk.clone | while | flops 1375991808 | bytes 119894808 | solution.py:250
  356.2 3.5 fusion.192
  359.7 2.4 fusion.193
  364.1 2.2 fusion.196
  366.3 3.1 fusion.194
  369.4 5.6 %fusion.195 = f32[1024,2,64]{0,2,1:T(8,128)} fusion(f32[2,512,2,1024]{3,1,2,0:T(8,128)} %copy-done.2, f32[2,2,512]{2,1,0:T(2,128)S(1)} %dynamic-slice_bitcast_fusion.3, pred[512,1024]{1,0:T(8,128)(4,1)S(1)} %compare_and_fusion.7, f32[1024,2,64]{0,2,1:T(8,128)} %get-tuple-element.598, pred[]{:T(512)S(6)} %compare.15, ...), kind=kOutput, calls=%fused_computation.40.clone.1.clone | convolution fusion | flops 277086208 | bytes 10231813 | tf_op jit(solution)/shard_map/while/body/eval_jaxpr/kgqs,qkgd->skd/dot_general | solution.py:241
  379.6 3.5 fusion.192
  383.9 2.4 fusion.193
  388.3 2.2 fusion.196
  390.5 3.2 fusion.194
  393.6 5.9 %fusion.195 = f32[1024,2,64]{0,2,1:T(8,128)} fusion(f32[2,512,2,1024]{3,1,2,0:T(8,128)} %copy-done.2, f32[2,2,512]{2,1,0:T(2,128)S(1)} %dynamic-slice_bitcast_fusion.3, pred[512,1024]{1,0:T(8,128)(4,1)S(1)} %compare_and_fusion.7, f32[1024,2,64]{0,2,1:T(8,128)} %get-tuple-element.598, pred[]{:T(512)S(6)} %compare.15, ...), kind=kOutput, calls=%fused_computation.40.clone.1.clone | convolution fusion | flops 277086208 | bytes 10231813 | tf_op jit(solution)/shard_map/while/body/eval_jaxpr/kgqs,qkgd->skd/dot_general | solution.py:241
  399.8 3.3 convolution_convert_fusion.13
  403.1 3.5 add_add_fusion.4
  406.6 3.0 copy.28
  409.6 3.2 reshape.329
  421.0 3.4 collective-permute-start.22
  424.4 2.3 convolution_convert_fusion.3
  426.8 2.3 convolution_convert_fusion.4
  429.1 26.1 %collective-permute-done.21 = bf16[256,1024]{1,0:T(8,128)(2,1)S(1)} collective-permute-done((bf16[256,1024]{1,0:T(8,128)(2,1)}, bf16[256,1024]{1,0:T(8,128)(2,1)S(1)}, u32[]{:S(2)}, u32[]{:S(2)}) %collective-permute-start.21) | collective-permute-done | bytes 524320 | tf_op jit(solution)/shard_map/ppermute | solution.py:77
  455.3 2.7 multiply_reduce_fusion.2
  460.6 4.4 convert_element_type.202
  465.0 2.5 convert_element_type.200
  467.8 2.5 convert_element_type.201
  471.7 2.2 collective-permute-done.26
  474.0 15.7 %all-reduce.9.cloned.1.call-done = (bf16[1024,512]{1,0:T(8,128)(2,1)}, bf16[256,1024]{1,0:T(8,128)(2,1)}) async-done(((bf16[1024,512]{1,0:T(8,128)(2,1)}, bf16[256,1024]{1,0:T(8,128)(2,1)}), (bf16[1024,512]{1,0:T(8,128)(2,1)}, bf16[256,1024]{1,0:T(8,128)(2,1)})) %all-reduce.9.cloned.1.call-update) | async-done | bytes 1572880 | tf_op jit(solution)/shard_map/psum | solution.py:286
  491.3 2.5 fusion.55
  493.8 2.5 collective-permute-start.28
  (298 shorter events, 81.0 us)
Async XLA Ops:
  7.2 204.3 %copy-start = (bf16[1024,1152]{1,0:T(8,128)(2,1)S(1)}, bf16[1024,1152]{1,0:T(8,128)(2,1)}, u32[]{:S(2)}) copy-start(bf16[1024,1152]{1,0:T(8,128)(2,1)} %param.30) | copy-start | bytes 7077892
  7.2 10.0 %copy-start.54 = (s32[1,1024]{1,0:T(1,128)S(1)}, s32[1,1024]{1,0:T(1,128)}, u32[]{:S(2)}) copy-start(s32[1,1024]{1,0:T(1,128)} %param.19) | copy-start | bytes 12292
  7.2 14.5 %copy-start.43 = (bf16[1024,128]{1,0:T(8,128)(2,1)S(1)}, bf16[1024,128]{1,0:T(8,128)(2,1)}, u32[]{:S(2)}) copy-start(bf16[1024,128]{1,0:T(8,128)(2,1)} %param.26) | copy-start | bytes 786436
  7.2 419.5 %all-reduce.11.cloned.1.call-start = ((), (), s32[]{:S(2)}) async-start(), calls=%async_computation.1 | async-start | bytes 14155776 | tf_op jit(solution)/shard_map/psum | solution.py:197
  8.8 9.6 %copy-start.57 = (f32[256]{0:T(256)}, f32[256]{0:T(256)S(1)}, u32[]{:S(2)}) copy-start(f32[256]{0:T(256)S(1)} %multiply_reduce_fusion.8) | copy-start | bytes 3076
  8.8 9.6 %copy-start.55 = (f32[256]{0:T(256)}, f32[256]{0:T(256)S(1)}, u32[]{:S(2)}) copy-start(f32[256]{0:T(256)S(1)} %fusion.96) | copy-start | bytes 3076
  10.2 19.7 %collective-permute-start = (bf16[256,1024]{1,0:T(8,128)(2,1)S(1)}, bf16[256,1024]{1,0:T(8,128)(2,1)}, u32[]{:S(2)}, u32[]{:S(2)}) collective-permute-start(bf16[256,1024]{1,0:T(8,128)(2,1)S(1)} %multiply_convert_fusion.3), channel_id=1, source_target_pairs={{0,1},{1,2},{2,3},{3,0},{4,5},{5,6},{6,7},{7,4},{8,9},{9,10},{10,1... | collective-permute-start | bytes 1572872 | tf_op jit(solution)/shard_map/ppermute | solution.py:68
  13.3 36.7 %collective-permute-start.1 = (bf16[256,1024]{1,0:T(8,128)(2,1)S(1)}, bf16[256,1024]{1,0:T(8,128)(2,1)}, u32[]{:S(2)}, u32[]{:S(2)}) collective-permute-start(bf16[256,1024]{1,0:T(8,128)(2,1)S(1)} %multiply_convert_fusion.3), channel_id=1, source_target_pairs={{0,2},{1,3},{2,0},{3,1},{4,6},{5,7},{6,4},{7,5},{8,10},{9,11},{10,... | collective-permute-start | bytes 1572872 | tf_op jit(solution)/shard_map/ppermute | solution.py:68
  15.9 34.1 %collective-permute-start.2 = (bf16[256,1024]{1,0:T(8,128)(2,1)S(1)}, bf16[256,1024]{1,0:T(8,128)(2,1)}, u32[]{:S(2)}, u32[]{:S(2)}) collective-permute-start(bf16[256,1024]{1,0:T(8,128)(2,1)S(1)} %multiply_convert_fusion.3), channel_id=1, source_target_pairs={{0,3},{1,0},{2,1},{3,2},{4,7},{5,4},{6,5},{7,6},{8,11},{9,8},{10,9... | collective-permute-start | bytes 1572872 | tf_op jit(solution)/shard_map/ppermute | solution.py:68
  29.3 22.1 %copy-start.11 = (bf16[1024,512]{1,0:T(8,128)(2,1)S(1)}, bf16[1024,512]{1,0:T(8,128)(2,1)}, u32[]{:S(2)}) copy-start(bf16[1024,512]{1,0:T(8,128)(2,1)} %constant_dynamic-update-slice_fusion) | copy-start | bytes 3145732
  29.9 38.7 %copy-start.24 = (f32[1024,32]{0,1:T(8,128)}, f32[1024,32]{0,1:T(8,128)S(1)}, u32[]{:S(2)}) copy-start(f32[1024,32]{0,1:T(8,128)S(1)} %get-tuple-element.321) | copy-start | bytes 393220
  29.9 38.7 %copy-start.26 = (f32[1024,32]{0,1:T(8,128)}, f32[1024,32]{0,1:T(8,128)S(1)}, u32[]{:S(2)}) copy-start(f32[1024,32]{0,1:T(8,128)S(1)} %get-tuple-element.322) | copy-start | bytes 393220
  51.5 16.4 %copy-start.59 = (f32[64]{0:T(128)S(1)}, f32[64]{0:T(128)}, u32[]{:S(2)}) copy-start(f32[64]{0:T(128)} %param.24) | copy-start | bytes 772
  52.8 15.4 %copy-start.5 = (f32[1024,512]{0,1:T(8,128)}, f32[1024,512]{0,1:T(8,128)S(1)}, u32[]{:S(2)}) copy-start(f32[1024,512]{0,1:T(8,128)S(1)} %fusion.107) | copy-start | bytes 6291460
  52.8 15.2 %copy-start.61 = (f32[64]{0:T(128)S(1)}, f32[64]{0:T(128)}, u32[]{:S(2)}) copy-start(f32[64]{0:T(128)} %param.23) | copy-start | bytes 772
  52.9 15.4 %copy-start.50 = (f32[1024,2]{0,1:T(2,128)}, f32[1024,2]{0,1:T(2,128)S(1)}, u32[]{:S(2)}) copy-start(f32[1024,2]{0,1:T(2,128)S(1)} %multiply_reduce_fusion.11) | copy-start | bytes 24580
  53.0 14.3 %copy-start.44 = (f32[1024,4]{0,1:T(4,128)}, f32[1024,4]{0,1:T(4,128)S(1)}, u32[]{:S(2)}) copy-start(f32[1024,4]{0,1:T(4,128)S(1)} %multiply_reduce_fusion.7) | copy-start | bytes 49156
  53.1 37.9 %collective-permute-start.3 = (bf16[256,1024]{1,0:T(8,128)(2,1)}, bf16[256,1024]{1,0:T(8,128)(2,1)}, u32[]{:S(2)}, u32[]{:S(2)}) collective-permute-start(bf16[256,1024]{1,0:T(8,128)(2,1)} %convert_element_type.158), channel_id=1, source_target_pairs={{0,1},{1,2},{2,3},{3,0},{4,5},{5,6},{6,7},{7,4},{8,9},{9,10},{10,1... | collective-permute-start | bytes 1572872 | tf_op jit(solution)/shard_map/ppermute | solution.py:68
  64.8 35.0 %collective-permute-start.4 = (bf16[256,1024]{1,0:T(8,128)(2,1)}, bf16[256,1024]{1,0:T(8,128)(2,1)}, u32[]{:S(2)}, u32[]{:S(2)}) collective-permute-start(bf16[256,1024]{1,0:T(8,128)(2,1)} %convert_element_type.158), channel_id=1, source_target_pairs={{0,2},{1,3},{2,0},{3,1},{4,6},{5,7},{6,4},{7,5},{8,10},{9,11},{10,... | collective-permute-start | bytes 1572872 | tf_op jit(solution)/shard_map/ppermute | solution.py:68
  66.4 33.4 %collective-permute-start.5 = (bf16[256,1024]{1,0:T(8,128)(2,1)}, bf16[256,1024]{1,0:T(8,128)(2,1)}, u32[]{:S(2)}, u32[]{:S(2)}) collective-permute-start(bf16[256,1024]{1,0:T(8,128)(2,1)} %convert_element_type.158), channel_id=1, source_target_pairs={{0,3},{1,0},{2,1},{3,2},{4,7},{5,4},{6,5},{7,6},{8,11},{9,8},{10,9... | collective-permute-start | bytes 1572872 | tf_op jit(solution)/shard_map/ppermute | solution.py:68
  90.9 13.5 %copy-start.14 = (bf16[1024,2,2,64]{0,3,2,1:T(8,128)(2,1)}, bf16[1024,2,2,64]{0,3,2,1:T(8,128)(2,1)S(1)}, u32[]{:S(2)}) copy-start(bf16[1024,2,2,64]{0,3,2,1:T(8,128)(2,1)S(1)} %get-tuple-element.635) | copy-start | bytes 1572868
  90.9 13.6 %copy-start.16 = (bf16[256,1024]{1,0:T(8,128)(2,1)S(1)}, bf16[256,1024]{1,0:T(8,128)(2,1)}, u32[]{:S(2)}) copy-start(bf16[256,1024]{1,0:T(8,128)(2,1)} %param.28) | copy-start | bytes 1572868
  107.9 35.0 %collective-permute-start.6 = (bf16[256,1024]{1,0:T(8,128)(2,1)}, bf16[256,1024]{1,0:T(8,128)(2,1)}, u32[]{:S(2)}, u32[]{:S(2)}) collective-permute-start(bf16[256,1024]{1,0:T(8,128)(2,1)} %convolution_convert_fusion.12), channel_id=1, source_target_pairs={{0,2},{1,3},{2,0},{3,1},{4,6},{5,7},{6,4},{7,5},{8,10},{9,11},{10,... | collective-permute-start | bytes 1572872 | tf_op jit(solution)/shard_map/ppermute | solution.py:77
  118.6 24.3 %collective-permute-start.7 = (bf16[256,1024]{1,0:T(8,128)(2,1)}, bf16[256,1024]{1,0:T(8,128)(2,1)}, u32[]{:S(2)}, u32[]{:S(2)}) collective-permute-start(bf16[256,1024]{1,0:T(8,128)(2,1)} %convolution_convert_fusion.11), channel_id=1, source_target_pairs={{0,3},{1,0},{2,1},{3,2},{4,7},{5,4},{6,5},{7,6},{8,11},{9,8},{10,9... | collective-permute-start | bytes 1572872 | tf_op jit(solution)/shard_map/ppermute | solution.py:77
  122.0 34.8 %collective-permute-start.8 = (bf16[256,1024]{1,0:T(8,128)(2,1)}, bf16[256,1024]{1,0:T(8,128)(2,1)}, u32[]{:S(2)}, u32[]{:S(2)}) collective-permute-start(bf16[256,1024]{1,0:T(8,128)(2,1)} %convolution_convert_fusion.10), channel_id=1, source_target_pairs={{0,1},{1,2},{2,3},{3,0},{4,5},{5,6},{6,7},{7,4},{8,9},{9,10},{10,1... | collective-permute-start | bytes 1572872 | tf_op jit(solution)/shard_map/ppermute | solution.py:77
  122.0 34.8 %copy-start.9 = (f32[256,1024]{1,0:T(8,128)S(1)}, f32[256,1024]{1,0:T(8,128)}, u32[]{:S(2)}) copy-start(f32[256,1024]{1,0:T(8,128)} %param.18) | copy-start | bytes 3145732
  122.0 34.8 %copy-start.17 = (bf16[256,1024]{1,0:T(8,128)(2,1)S(1)}, bf16[256,1024]{1,0:T(8,128)(2,1)}, u32[]{:S(2)}) copy-start(bf16[256,1024]{1,0:T(8,128)(2,1)} %param.28) | copy-start | bytes 1572868
  122.0 36.7 %copy-start.52 = (f32[1024]{0:T(1024)S(1)}, f32[1024]{0:T(1024)}, u32[]{:S(2)}) copy-start(f32[1024]{0:T(1024)} %param.22) | copy-start | bytes 12292
  122.0 50.1 %copy-start.28 = (bf16[1152,1024]{1,0:T(8,128)(2,1)S(1)}, bf16[1152,1024]{1,0:T(8,128)(2,1)}, u32[]{:S(2)}) copy-start(bf16[1152,1024]{1,0:T(8,128)(2,1)} %param.31) | copy-start | bytes 7077892
  122.0 50.1 %copy-start.38 = (bf16[1024,1024]{1,0:T(8,128)(2,1)S(1)}, bf16[1024,1024]{1,0:T(8,128)(2,1)}, u32[]{:S(2)}) copy-start(bf16[1024,1024]{1,0:T(8,128)(2,1)} %pad_maximum_fusion.1) | copy-start | bytes 6291460
  158.7 113.9 %copy-start.7 = (f32[256,1024]{1,0:T(8,128)}, f32[256,1024]{1,0:T(8,128)S(1)}, u32[]{:S(2)}) copy-start(f32[256,1024]{1,0:T(8,128)S(1)} %get-tuple-element.324) | copy-start | bytes 3145732
  158.9 46.5 %copy-start.4 = (bf16[1024,1152]{1,0:T(8,128)(2,1)S(1)}, bf16[1024,1152]{1,0:T(8,128)(2,1)}, u32[]{:S(2)}) copy-start(bf16[1024,1152]{1,0:T(8,128)(2,1)} %param.29) | copy-start | bytes 7077892
  158.9 35.3 %collective-permute-start.10 = (bf16[256,1024]{1,0:T(8,128)(2,1)S(1)}, bf16[256,1024]{1,0:T(8,128)(2,1)S(1)}, u32[]{:S(2)}, u32[]{:S(2)}) collective-permute-start(bf16[256,1024]{1,0:T(8,128)(2,1)S(1)} %multiply_convert_fusion.2), channel_id=1, source_target_pairs={{0,2},{1,3},{2,0},{3,1},{4,6},{5,7},{6,4},{7,5},{8,10},{9,11},{10,... | collective-permute-start | bytes 1572872 | tf_op jit(solution)/shard_map/ppermute | solution.py:68
  169.6 35.8 %collective-permute-start.11 = (bf16[256,1024]{1,0:T(8,128)(2,1)S(1)}, bf16[256,1024]{1,0:T(8,128)(2,1)S(1)}, u32[]{:S(2)}, u32[]{:S(2)}) collective-permute-start(bf16[256,1024]{1,0:T(8,128)(2,1)S(1)} %multiply_convert_fusion.2), channel_id=1, source_target_pairs={{0,3},{1,0},{2,1},{3,2},{4,7},{5,4},{6,5},{7,6},{8,11},{9,8},{10,9... | collective-permute-start | bytes 1572872 | tf_op jit(solution)/shard_map/ppermute | solution.py:68
  170.0 35.3 %collective-permute-start.9 = (bf16[256,1024]{1,0:T(8,128)(2,1)S(1)}, bf16[256,1024]{1,0:T(8,128)(2,1)S(1)}, u32[]{:S(2)}, u32[]{:S(2)}) collective-permute-start(bf16[256,1024]{1,0:T(8,128)(2,1)S(1)} %multiply_convert_fusion.2), channel_id=1, source_target_pairs={{0,1},{1,2},{2,3},{3,0},{4,5},{5,6},{6,7},{7,4},{8,9},{9,10},{10,1... | collective-permute-start | bytes 1572872 | tf_op jit(solution)/shard_map/ppermute | solution.py:68
  219.6 76.5 %copy-start.46 = (bf16[1024,1152]{1,0:T(8,128)(2,1)}, bf16[1024,1152]{1,0:T(8,128)(2,1)S(1)}, u32[]{:S(2)}) copy-start(bf16[1024,1152]{1,0:T(8,128)(2,1)S(1)} %get-tuple-element.176) | copy-start | bytes 7077892
  224.0 33.7 %collective-permute-start.12 = (bf16[256,1024]{1,0:T(8,128)(2,1)S(1)}, bf16[256,1024]{1,0:T(8,128)(2,1)S(1)}, u32[]{:S(2)}, u32[]{:S(2)}) collective-permute-start(bf16[256,1024]{1,0:T(8,128)(2,1)S(1)} %fusion.50), channel_id=1, source_target_pairs={{0,2},{1,3},{2,0},{3,1},{4,6},{5,7},{6,4},{7,5},{8,10},{9,11},{10,... | collective-permute-start | bytes 1572872 | tf_op jit(solution)/shard_map/ppermute | solution.py:77
  234.6 23.1 %collective-permute-start.13 = (bf16[256,1024]{1,0:T(8,128)(2,1)S(1)}, bf16[256,1024]{1,0:T(8,128)(2,1)S(1)}, u32[]{:S(2)}, u32[]{:S(2)}) collective-permute-start(bf16[256,1024]{1,0:T(8,128)(2,1)S(1)} %fusion.51), channel_id=1, source_target_pairs={{0,3},{1,0},{2,1},{3,2},{4,7},{5,4},{6,5},{7,6},{8,11},{9,8},{10,9... | collective-permute-start | bytes 1572872 | tf_op jit(solution)/shard_map/ppermute | solution.py:77
  238.9 32.4 %collective-permute-start.14 = (bf16[256,1024]{1,0:T(8,128)(2,1)S(1)}, bf16[256,1024]{1,0:T(8,128)(2,1)S(1)}, u32[]{:S(2)}, u32[]{:S(2)}) collective-permute-start(bf16[256,1024]{1,0:T(8,128)(2,1)S(1)} %fusion.52), channel_id=1, source_target_pairs={{0,1},{1,2},{2,3},{3,0},{4,5},{5,6},{6,7},{7,4},{8,9},{9,10},{10,1... | collective-permute-start | bytes 1572872 | tf_op jit(solution)/shard_map/ppermute | solution.py:77
  247.7 24.9 %copy-start.20 = (f32[256,1024]{1,0:T(8,128)S(1)}, f32[256,1024]{1,0:T(8,128)}, u32[]{:S(2)}) copy-start(f32[256,1024]{1,0:T(8,128)} %param.20) | copy-start | bytes 3145732
  274.0 32.5 %collective-permute-start.15 = (bf16[256,1024]{1,0:T(8,128)(2,1)}, bf16[256,1024]{1,0:T(8,128)(2,1)}, u32[]{:S(2)}, u32[]{:S(2)}) collective-permute-start(bf16[256,1024]{1,0:T(8,128)(2,1)} %get-tuple-element.298), channel_id=1, source_target_pairs={{0,1},{1,2},{2,3},{3,0},{4,5},{5,6},{6,7},{7,4},{8,9},{9,10},{10,1... | collective-permute-start | bytes 1572872 | tf_op jit(solution)/shard_map/ppermute | solution.py:68
  293.8 25.1 %collective-permute-start.16 = (bf16[256,1024]{1,0:T(8,128)(2,1)}, bf16[256,1024]{1,0:T(8,128)(2,1)}, u32[]{:S(2)}, u32[]{:S(2)}) collective-permute-start(bf16[256,1024]{1,0:T(8,128)(2,1)} %get-tuple-element.298), channel_id=1, source_target_pairs={{0,2},{1,3},{2,0},{3,1},{4,6},{5,7},{6,4},{7,5},{8,10},{9,11},{10,... | collective-permute-start | bytes 1572872 | tf_op jit(solution)/shard_map/ppermute | solution.py:68
  293.8 33.5 %collective-permute-start.17 = (bf16[256,1024]{1,0:T(8,128)(2,1)}, bf16[256,1024]{1,0:T(8,128)(2,1)}, u32[]{:S(2)}, u32[]{:S(2)}) collective-permute-start(bf16[256,1024]{1,0:T(8,128)(2,1)} %get-tuple-element.298), channel_id=1, source_target_pairs={{0,3},{1,0},{2,1},{3,2},{4,7},{5,4},{6,5},{7,6},{8,11},{9,8},{10,9... | collective-permute-start | bytes 1572872 | tf_op jit(solution)/shard_map/ppermute | solution.py:68
  300.1 28.9 %copy-start.29 = (bf16[1152,1024]{1,0:T(8,128)(2,1)S(1)}, bf16[1152,1024]{1,0:T(8,128)(2,1)}, u32[]{:S(2)}) copy-start(bf16[1152,1024]{1,0:T(8,128)(2,1)} %param.31) | copy-start | bytes 7077892
  300.1 189.6 %all-reduce.9.cloned.1.call-start = ((), (), s32[]{:S(2)}) async-start(), calls=%async_computation | async-start | bytes 3145728 | tf_op jit(solution)/shard_map/psum | solution.py:286
  329.0 21.8 %copy-start.39 = (bf16[1024,1024]{1,0:T(8,128)(2,1)}, bf16[1024,1024]{1,0:T(8,128)(2,1)S(1)}, u32[]{:S(2)}) copy-start(bf16[1024,1024]{1,0:T(8,128)(2,1)S(1)} %pad_maximum_fusion.3) | copy-start | bytes 6291460
  334.1 16.7 %copy-start.18 = (bf16[256,1024]{1,0:T(8,128)(2,1)S(1)}, bf16[256,1024]{1,0:T(8,128)(2,1)}, u32[]{:S(2)}) copy-start(bf16[256,1024]{1,0:T(8,128)(2,1)} %param.28) | copy-start | bytes 1572868
  335.7 15.8 %copy-start.15 = (bf16[1024,2,2,64]{0,3,2,1:T(8,128)(2,1)S(1)}, bf16[1024,2,2,64]{0,3,2,1:T(8,128)(2,1)}, u32[]{:S(2)}) copy-start(bf16[1024,2,2,64]{0,3,2,1:T(8,128)(2,1)} %copy-done.14) | copy-start | bytes 1572868
  335.7 67.3 %collective-permute-start.18 = (bf16[256,1024]{1,0:T(8,128)(2,1)}, bf16[256,1024]{1,0:T(8,128)(2,1)}, u32[]{:S(2)}, u32[]{:S(2)}) collective-permute-start(bf16[256,1024]{1,0:T(8,128)(2,1)} %convolution_convert_fusion.9), channel_id=1, source_target_pairs={{0,2},{1,3},{2,0},{3,1},{4,6},{5,7},{6,4},{7,5},{8,10},{9,11},{10,... | collective-permute-start | bytes 1572872 | tf_op jit(solution)/shard_map/ppermute | solution.py:77
  339.3 63.8 %collective-permute-start.19 = (bf16[256,1024]{1,0:T(8,128)(2,1)}, bf16[256,1024]{1,0:T(8,128)(2,1)}, u32[]{:S(2)}, u32[]{:S(2)}) collective-permute-start(bf16[256,1024]{1,0:T(8,128)(2,1)} %convolution_convert_fusion.8), channel_id=1, source_target_pairs={{0,3},{1,0},{2,1},{3,2},{4,7},{5,4},{6,5},{7,6},{8,11},{9,8},{10,9... | collective-permute-start | bytes 1572872 | tf_op jit(solution)/shard_map/ppermute | solution.py:77
  350.1 52.9 %collective-permute-start.20 = (bf16[256,1024]{1,0:T(8,128)(2,1)}, bf16[256,1024]{1,0:T(8,128)(2,1)}, u32[]{:S(2)}, u32[]{:S(2)}) collective-permute-start(bf16[256,1024]{1,0:T(8,128)(2,1)} %convolution_convert_fusion.7), channel_id=1, source_target_pairs={{0,1},{1,2},{2,3},{3,0},{4,5},{5,6},{6,7},{7,4},{8,9},{9,10},{10,1... | collective-permute-start | bytes 1572872 | tf_op jit(solution)/shard_map/ppermute | solution.py:77
  351.5 48.3 %copy-start.35 = (bf16[32,8,2,512]{3,1,2,0:T(8,128)(2,1)S(1)}, bf16[32,8,2,512]{3,1,2,0:T(8,128)(2,1)}, u32[]{:S(2)}) copy-start(bf16[32,8,2,512]{3,1,2,0:T(8,128)(2,1)} %copy-done.34) | copy-start | bytes 1572868
  418.5 36.7 %collective-permute-start.21 = (bf16[256,1024]{1,0:T(8,128)(2,1)}, bf16[256,1024]{1,0:T(8,128)(2,1)S(1)}, u32[]{:S(2)}, u32[]{:S(2)}) collective-permute-start(bf16[256,1024]{1,0:T(8,128)(2,1)} %convolution_convert_fusion.6), channel_id=1, source_target_pairs={{0,2},{1,3},{2,0},{3,1},{4,6},{5,7},{6,4},{7,5},{8,10},{9,11},{10,... | collective-permute-start | bytes 1572872 | tf_op jit(solution)/shard_map/ppermute | solution.py:77
  421.0 34.2 %collective-permute-start.22 = (bf16[256,1024]{1,0:T(8,128)(2,1)}, bf16[256,1024]{1,0:T(8,128)(2,1)S(1)}, u32[]{:S(2)}, u32[]{:S(2)}) collective-permute-start(bf16[256,1024]{1,0:T(8,128)(2,1)} %convolution_convert_fusion.5), channel_id=1, source_target_pairs={{0,3},{1,0},{2,1},{3,2},{4,7},{5,4},{6,5},{7,6},{8,11},{9,8},{10,9... | collective-permute-start | bytes 1572872 | tf_op jit(solution)/shard_map/ppermute | solution.py:77
  426.8 28.5 %copy-start.10 = (f32[256,1024]{1,0:T(8,128)S(1)}, f32[256,1024]{1,0:T(8,128)}, u32[]{:S(2)}) copy-start(f32[256,1024]{1,0:T(8,128)} %param.18) | copy-start | bytes 3145732
  426.8 28.5 %copy-start.53 = (f32[1024]{0:T(1024)S(1)}, f32[1024]{0:T(1024)}, u32[]{:S(2)}) copy-start(f32[1024]{0:T(1024)} %param.21) | copy-start | bytes 12292
  426.8 28.5 %copy-start.56 = (f32[256]{0:T(256)S(1)}, f32[256]{0:T(256)}, u32[]{:S(2)}) copy-start(f32[256]{0:T(256)} %copy-done.55) | copy-start | bytes 3076
  429.1 26.2 %collective-permute-start.23 = (bf16[256,1024]{1,0:T(8,128)(2,1)}, bf16[256,1024]{1,0:T(8,128)(2,1)}, u32[]{:S(2)}, u32[]{:S(2)}) collective-permute-start(bf16[256,1024]{1,0:T(8,128)(2,1)} %convolution_convert_fusion.4), channel_id=1, source_target_pairs={{0,1},{1,2},{2,3},{3,0},{4,5},{5,6},{6,7},{7,4},{8,9},{9,10},{10,1... | collective-permute-start | bytes 1572872 | tf_op jit(solution)/shard_map/ppermute | solution.py:77
  458.1 1.2 collective-permute-start.24
  459.3 11.0 %collective-permute-start.25 = (f32[2176]{0:T(1024)S(1)}, f32[2176]{0:T(1024)S(1)}, u32[]{:S(2)}, u32[]{:S(2)}) collective-permute-start(f32[2176]{0:T(1024)S(1)} %add.248), channel_id=1, source_target_pairs={{0,8},{4,12},{8,0},{12,4},{16,24},{20,28},{24,16},{28,20},{1,9},{5... | collective-permute-start | bytes 26120 | tf_op jit(solution)/shard_map/ppermute | solution.py:85
  467.8 23.6 %copy-start.19 = (f32[256,1024]{1,0:T(8,128)S(1)}, f32[256,1024]{1,0:T(8,128)}, u32[]{:S(2)}) copy-start(f32[256,1024]{1,0:T(8,128)} %get-tuple-element.299) | copy-start | bytes 3145732
  470.3 3.7 collective-permute-start.26
  489.7 4.1 collective-permute-start.27
  493.8 5.6 %collective-permute-start.28 = (f32[2176]{0:T(1024)S(1)}, f32[2176]{0:T(1024)S(1)}, u32[]{:S(2)}, u32[]{:S(2)}) collective-permute-start(f32[2176]{0:T(1024)S(1)} %add.251), channel_id=1, source_target_pairs={{0,2},{1,3},{2,0},{3,1},{4,6},{5,7},{6,4},{7,5},{8,10},{9,11},{10,... | collective-permute-start | bytes 26120 | tf_op jit(solution)/shard_map/ppermute | solution.py:85
  (34 other events, 121.1 us)
Sparse Core Ops, SparseCore 0:
  300.2 112.9 all-reduce.10
  429.2 60.4 all-reduce.8
